TPU v7x, 128 devices: a whole 4x4x4 slice. The times are simulated.
128 devices in a mesh: group: 8 (over y_hi, x), slab: 16 (over z, y_lo, core).
Axes of the slice: x: 4, y: 4 (y_hi: 2, y_lo: 2; y = y_hi * 2 + y_lo), z: 4, core: 2. Of those that a mesh axis runs over, the one named last changes fastest.
Arguments:
- velocity: float32 [3, 128, 128, 2048], P(None, None, None, ('group', 'slab')), may hold values from -30 to 30
- register: float32 [3, 128, 128, 2048], P(None, None, None, ('group', 'slab')), may hold values from -4 to 4
- past: float32 [7, 512, 32, 96], P(None, ('group', 'slab')), may hold values from -4 to 4
- basis: float32 [16, 8, 256, 12288], P('slab', 'group'), may hold values from -6 to 6
- owner: int32 [16, 8], replicated, may hold values from 0 to 7, each once within a row
Outputs:
- new_velocity: float32 [3, 128, 128, 2048], P(None, None, None, ('group', 'slab'))
- new_register: float32 [3, 128, 128, 2048], P(None, None, None, ('group', 'slab'))
- coeffs: float32 [256, 8], replicated
- factor: float32 [8, 8], replicated
- directions: float32 [16, 8, 8, 12288], P('slab', 'group')
Inputs may be any that keep to these rules, and one draw needn't show every extreme that they name: Each row of owner names every group once.
All inputs are finite; a program needn't handle non-finite values.
Results may differ from a plain program's by a relative error of at most 0.000075.
Values sent between devices are 32-bit elements; how exact they have to be, the bound alone decides.
A program may use at most 256 MiB of HBM per device.

v0:
```python
import jax
import jax.numpy as jnp
from jax import lax
from jax.sharding import PartitionSpec as P

first_coef = (0.8, -0.2, 4.0 / 105.0, -1.0 / 280.0)
second_coef = (-205.0 / 72.0, 1.6, -0.2, 8.0 / 315.0, -1.0 / 560.0)
time_step = 0.02
viscosity = 0.4
section_decay = -5.0 / 9.0
section_gain = 15.0 / 16.0
reach = 4


def padded_2(block, sides, width):
    for axis, dim in sides:
        count = lax.axis_size(axis)
        forward = [(i, i + 1) for i in range(count - 1)]
        forward.append((count - 1, 0))
        backward = [(target, source) for source, target in forward]
        low = lax.ppermute(
            lax.slice_in_dim(block, block.shape[dim] - width, None, axis=dim), axis, forward
        )
        high = lax.ppermute(lax.slice_in_dim(block, 0, width, axis=dim), axis, backward)
        block = jnp.concatenate([low, block, high], axis=dim)
    return block


def difference(shifted, center):
    first = first_coef[0] * (shifted(1) - shifted(-1))
    for offset in range(2, 5):
        first = first + first_coef[offset - 1] * (shifted(offset) - shifted(-offset))
    second = second_coef[0] * center
    for offset in range(1, 5):
        second = second + second_coef[offset] * (shifted(offset) + shifted(-offset))
    return (first, second)


def axis_term(velocity, component, shifted):
    first, second = difference(shifted, velocity)
    return viscosity * second - velocity[component][None] * first


def coarsen(field):
    comps, wide_x, wide_y, wide_z = field.shape
    boxes = field.reshape(comps, wide_x // 4, 4, wide_y // 4, 4, wide_z // 4, 4).mean(
        axis=(2, 4, 6)
    )
    return boxes.transpose(3, 1, 0, 2).reshape(wide_z // 4, wide_x // 4, comps * (wide_y // 4))


def arrange(snaps, order):
    count, depth, across, lanes = snaps.shape
    groups = order.shape[0]
    pieces = snaps.reshape(count, depth, groups, across // groups, lanes)
    return jnp.take(pieces, order, axis=2)


def settle(moved):
    return moved.reshape(moved.shape[0], -1)


def tri_solve(lower_mat, rhs, transposed):
    return lax.linalg.triangular_solve(
        lower_mat, rhs, left_side=True, lower=True, transpose_a=transposed
    )


def inner(left, right):
    return lax.dot_general(
        left,
        right,
        (((1,), (1,)), ((), ())),
        precision=lax.Precision.HIGHEST,
        preferred_element_type=jnp.float32,
    )


def solve_coeffs(gram, proj):
    chol = jnp.linalg.cholesky(gram)
    return tri_solve(chol, tri_solve(chol, proj, False), True)


def local(velocity, register, past, basis, owner):
    width_z = velocity.shape[3]
    slab_index = lax.axis_index("slab")
    owner_row = lax.dynamic_index_in_dim(owner, slab_index, 0, keepdims=False)
    order = jnp.argsort(owner_row)

    def shift_x(offset):
        return jnp.roll(velocity, -offset, axis=1)

    def shift_y(offset):
        return jnp.roll(velocity, -offset, axis=2)

    padded = padded_2(velocity, ((("group", "slab"), 3),), reach)
    term_x = axis_term(velocity, 0, shift_x)
    term_y = axis_term(velocity, 1, shift_y)
    term_z = axis_term(
        velocity, 2, lambda offset: padded[:, :, :, reach + offset : reach + offset + width_z]
    )
    tendency = term_x + term_y + term_z
    new_register = section_decay * register + time_step * tendency
    new_velocity = velocity + section_gain * new_register
    fresh = coarsen(new_velocity)[None]
    together = jnp.concatenate([past, fresh], axis=0)
    rows = settle(
        lax.all_to_all(arrange(together, order), "group", split_axis=2, concat_axis=2, tiled=True)
    )
    blocks = basis.reshape(basis.shape[2], basis.shape[3])
    total = float(rows.shape[1] * lax.axis_size("group") * lax.axis_size("slab"))
    proj_local = inner(blocks, rows) / total
    gram_local = inner(blocks, blocks) / total
    proj, gram = lax.psum((proj_local, gram_local), ("group", "slab"))
    coeffs = solve_coeffs(gram, proj)
    residual = rows - lax.dot_general(
        coeffs,
        blocks,
        (((0,), (0,)), ((), ())),
        precision=lax.Precision.HIGHEST,
        preferred_element_type=jnp.float32,
    )
    wgram = lax.psum(inner(residual, residual) / total, ("group", "slab"))
    factor = jnp.linalg.cholesky(wgram)
    directions = tri_solve(factor, residual, False)
    return (
        new_velocity,
        new_register,
        coeffs,
        factor,
        directions.reshape(1, 1, directions.shape[0], directions.shape[1]),
    )


def solution(mesh):
    in_specs = (
        P(None, None, None, ("group", "slab")),
        P(None, None, None, ("group", "slab")),
        P(None, ("group", "slab"), None, None),
        P("slab", "group", None, None),
        P(),
    )
    out_specs = (
        P(None, None, None, ("group", "slab")),
        P(None, None, None, ("group", "slab")),
        P(),
        P(),
        P("slab", "group", None, None),
    )
    return jax.shard_map(local, mesh=mesh, in_specs=in_specs, out_specs=out_specs, check_vma=False)
```

profile of v0, /device:TPU:1, one launch (start us, length us, event | category | flops | bytes accessed | tf_op | source)
XLA Modules:
  0.0 595.7 jit_solution(9318567299556431908)
XLA Ops:
  7.2 2.2 fusion.52
  9.4 1.0 copy.39
  10.3 2.7 collective-permute-start.1
  13.0 1.0 copy.38
  14.0 15.2 %fusion.13 = f32[256,256]{0,1:T(8,128)} fusion(f32[1,1,256,12288]{3,2,1,0:T(8,128)} %param.8), kind=kOutput, calls=%fused_computation.44 | convolution fusion | flops 9663741952 | bytes 12845056 | tf_op jit(solution)/shard_map/dot_general | solution.py:70
  29.3 1.8 slice_bitcast_fusion.2
  31.1 1.9 constant_dynamic-update-slice_fusion
  33.0 3.8 fusion.50
  36.7 3.8 fusion.51
  40.5 3.6 fusion.48
  44.1 3.8 fusion.49
  47.9 3.7 fusion.46
  51.6 3.7 fusion.47
  55.3 3.7 fusion.44
  59.0 3.8 fusion.45
  62.8 3.2 fusion.42
  66.7 3.1 fusion.40
  70.4 3.1 fusion.38
  74.2 3.1 fusion.36
  78.1 1.0 sort.17
  79.1 2.1 copy.29
  81.2 93.0 %all-reduce.3.cloned.1.call-done = f32[256,256]{0,1:T(8,128)} async-done(((f32[256,256]{0,1:T(8,128)}), f32[256,256]{0,1:T(8,128)}) %all-reduce.3.cloned.1.call-update) | async-done | bytes 262160 | tf_op jit(solution)/shard_map/psum | solution.py:114
  174.2 1.1 copy.28
  175.3 1.0 fusion.22
  177.0 11.9 %cholesky.64 = f32[128,128]{1,0:T(8,128)S(1)} custom-call(f32[128,128]{1,0:T(8,128)S(1)} %cholesky.156), custom_call_target="Cholesky" | custom-call | tf_op jit(solution)/shard_map/jit(cholesky)/cholesky | solution.py:80
  191.0 11.3 %custom-call.22 = f32[1,128,128]{1,2,0:T(8,128)} custom-call(f32[1,128,128]{2,1,0:T(8,128)} %get-tuple-element.69), custom_call_target="InvertDiagBlocksLowerTriangular" | custom-call | tf_op jit(solution)/shard_map/jit(cholesky)/cholesky | solution.py:80
  202.3 1.1 constant_dynamic-update-slice_fusion.1
  203.3 1.7 convolution_subtract_fusion.1
  205.1 13.2 %cholesky.132 = f32[128,128]{1,0:T(8,128)} custom-call(f32[128,128]{1,0:T(8,128)} %convolution_subtract_fusion.1), custom_call_target="Cholesky" | custom-call | tf_op jit(solution)/shard_map/jit(cholesky)/cholesky | solution.py:80
  221.1 1.1 select_select_fusion
  222.3 1.6 copy.26
  223.9 2.5 copy_dynamic-update-slice_fusion
  226.5 34.3 %multiply_add_fusion = (f32[3,128,128,16]{2,3,1,0:T(8,128)}, f32[3,128,128,16]{2,3,1,0:T(8,128)}) fusion(f32[3,128,128,16]{2,3,1,0:T(8,128)S(1)} %copy-done.2, f32[128,128,16]{1,2,0:T(8,128)} %get-tuple-element.47, f32[3,128,128,4]{2,3,1,0:T(4,128)S(1)} %copy.26, f32[3,128,128,20]{2,3,1,0:T(8,128)} %copy_dynamic-update-slice_fusion, ...), kind=kLoop, calls=%fused_computation.36 | loop fusion | flops 83361792 | bytes 79429632 | tf_op jit(solution)/shard_map/add | solution.py:104
  260.8 106.3 %reshape.61 = f32[3,32,4,32,4,4,4]{4,3,6,5,2,1,0:T(8,128)} reshape(f32[3,128,128,16]{2,3,1,0:T(8,128)} %get-tuple-element.25) | data formatting | bytes 6291456 | tf_op jit(solution)/shard_map/reshape | solution.py:46
  367.1 30.8 %reduce_sum.9 = f32[3,32,32,4]{2,3,1,0:T(4,128)S(1)} reduce(f32[3,32,4,32,4,4,4]{4,3,6,5,2,1,0:T(8,128)} %reshape.61, f32[]{:T(128)} %constant.167.clone.1), dimensions={2,4,6}, to_apply=%region_6.7 | reduce | flops 774144 | bytes 3194884 | tf_op jit(solution)/shard_map/reduce_sum | solution.py:46
  398.9 0.9 select_bitcast_fusion
  399.8 4.6 all-to-all-start
  404.5 5.2 while.1
  405.1 2.0 bitcast_dynamic-update-slice_fusion.2
  407.7 2.0 bitcast_dynamic-update-slice_fusion.2
  409.7 20.5 %custom-call.23 = f32[2,128,128]{1,2,0:T(8,128)S(1)} custom-call(f32[2,128,128]{2,1,0:T(8,128)} %get-tuple-element.14), custom_call_target="InvertDiagBlocksLowerTriangular" | custom-call | tf_op jit(solution)/shard_map/triangular_solve | solution.py:64
  430.8 12.7 %fusion.19 = f32[256,8]{0,1:T(8,128)S(1)} fusion(f32[8,12288]{1,0:T(8,128)S(1)} %reshape.62, f32[1,1,256,12288]{3,2,1,0:T(8,128)} %param.8), kind=kOutput, calls=%fused_computation.47 | convolution fusion | flops 301991936 | bytes 12984320 | tf_op jit(solution)/shard_map/dot_general | solution.py:70
  443.6 65.6 %psum.22 = f32[256,8]{0,1:T(8,128)S(1)} all-reduce(f32[256,8]{0,1:T(8,128)S(1)} %fusion.19), channel_id=1, replica_groups=mesh['group'=8,'slab'=16] {'group','slab'}, use_global_device_ids=true, to_apply=%region_7.8 | all-reduce | flops 2048 | bytes 16384 | tf_op jit(solution)/shard_map/psum | solution.py:114
  510.4 8.9 %convolution_subtract_fusion = f32[8,12288]{1,0:T(8,128)S(1)} fusion(f32[8,12288]{1,0:T(8,128)S(1)} %reshape.62, f32[256,8]{0,1:T(8,128)S(1)} %pad_maximum_fusion.18, f32[1,1,256,12288]{3,2,1,0:T(8,128)} %param.8), kind=kOutput, calls=%fused_computation.4 | convolution fusion | flops 302088192 | bytes 13377536 | tf_op jit(solution)/shard_map/dot_general | solution.py:116
  519.4 0.9 convolution_multiply_fusion
  520.3 63.7 %psum.23 = f32[8,8]{0,1:T(8,128)S(1)} all-reduce(f32[8,8]{0,1:T(8,128)S(1)} %convolution_multiply_fusion), channel_id=1, replica_groups=mesh['group'=8,'slab'=16] {'group','slab'}, use_global_device_ids=true, to_apply=%region_8.9 | all-reduce | flops 64 | bytes 512 | tf_op jit(solution)/shard_map/psum | solution.py:123
  585.4 1.2 select_bitcast_fusion.2
  587.3 1.3 convolution_bitcast_fusion
  (71 shorter events, 13.4 us)
Async XLA Ops:
  7.2 70.8 %copy-start = (s32[16,8]{0,1:T(8,128)S(1)}, s32[16,8]{0,1:T(8,128)}, u32[]{:S(2)}) copy-start(s32[16,8]{0,1:T(8,128)} %param.9) | copy-start | bytes 1540
  7.2 167.0 %all-reduce.3.cloned.1.call-start = ((), (), s32[]{:S(2)}) async-start(), calls=%async_computation.1 | async-start | bytes 524288 | tf_op jit(solution)/shard_map/psum | solution.py:114
  10.3 211.9 %collective-permute-start.1 = (f32[3,128,128,4]{2,1,3,0:T(8,128)}, f32[3,128,128,4]{2,1,3,0:T(8,128)}, u32[]{:S(2)}, u32[]{:S(2)}) collective-permute-start(f32[3,128,128,4]{2,1,3,0:T(8,128)} %copy.39), channel_id=1, source_target_pairs={{0,1},{1,2},{2,3},{3,4},{4,5},{5,6},{6,7},{7,8},{8,9},{9,10},{10,1... | collective-permute-start | bytes 2359304 | tf_op jit(solution)/shard_map/ppermute | solution.py:21
  14.0 15.3 %copy-start.2 = (f32[3,128,128,16]{2,3,1,0:T(8,128)S(1)}, f32[3,128,128,16]{2,3,1,0:T(8,128)}, u32[]{:S(2)}) copy-start(f32[3,128,128,16]{2,3,1,0:T(8,128)} %param.5) | copy-start | bytes 9437188
  14.0 209.9 %collective-permute-start = (f32[3,128,128,4]{2,1,3,0:T(8,128)}, f32[3,128,128,4]{2,1,3,0:T(8,128)}, u32[]{:S(2)}, u32[]{:S(2)}) collective-permute-start(f32[3,128,128,4]{2,1,3,0:T(8,128)} %copy.38), channel_id=1, source_target_pairs={{1,0},{2,1},{3,2},{4,3},{5,4},{6,5},{7,6},{8,7},{9,8},{10,9},{11,1... | collective-permute-start | bytes 2359304 | tf_op jit(solution)/shard_map/ppermute | solution.py:24
  176.3 0.7 copy-start.6
  188.9 0.6 copy-start.10
  219.1 1.9 copy-start.5
  221.1 5.4 copy-start.3
  221.1 5.4 copy-start.7
  221.1 5.4 copy-start.8
  221.1 5.4 copy-start.9
  367.0 31.2 %copy-start.4 = (f32[7,4,32,96]{3,0,2,1:T(8,128)S(1)}, f32[7,4,32,96]{3,0,2,1:T(8,128)}, u32[]{:S(2)}) copy-start(f32[7,4,32,96]{3,0,2,1:T(8,128)} %copy.29) | copy-start | bytes 1032196
  399.8 30.4 %all-to-all-start = ((f32[8,4,8,4,96]{4,0,3,1,2:T(8,128)}), f32[8,4,8,4,96]{4,0,3,1,2:T(8,128)S(1)}, u32[]{:S(2)}, u32[]{:S(2)}) async-start(f32[8,4,8,4,96]{4,0,3,1,2:T(8,128)} %select_bitcast_fusion), calls=%async_computation | async-start | bytes 1048576 | tf_op jit(solution)/shard_map/all_to_all | solution.py:108
  510.4 9.0 %copy-start.11 = (f32[256,8]{0,1:T(8,128)}, f32[256,8]{0,1:T(8,128)S(1)}, u32[]{:S(2)}) copy-start(f32[256,8]{0,1:T(8,128)S(1)} %pad_maximum_fusion.18) | copy-start | bytes 24580
  510.4 78.2 %copy-start.1 = (s32[16,8]{0,1:T(8,128)S(1)}, s32[16,8]{0,1:T(8,128)}, u32[]{:S(2)}) copy-start(s32[16,8]{0,1:T(8,128)} %param.9) | copy-start | bytes 1540
Sparse Core Ops, SparseCore 0:
  29.4 144.7 all-reduce.2
where the time goes:
time: 600 us; the launch traced here: 596 us
  local copies, waits for them, and re-layouts  176 us (29%)
  other arithmetic  132 us (22%)
  blocking collectives  129 us (22%)
  waiting for transfers between devices  93 us (16%)
  matrix products  43.1 us (7%)
  between operations  15.8 us (3%)
  starting transfers between devices  7.35 us (1%)
    reshape x1, local copies, waits for them, and re-layouts, coarsen(): field.reshape(comps, wide_x // 4, 4, wide_y // 4, 4, wide_z // 4, 4)  106 us
    psum x1, waiting for transfers between devices, local(): proj, gram = lax.psum((proj_local, gram_local), ('group', 'slab'))  93 us
    psum x1, blocking collectives, local(): proj, gram = lax.psum((proj_local, gram_local), ('group', 'slab'))  65.6 us
    psum x1, blocking collectives, local(): wgram = lax.psum(inner(residual, residual) / total, ('group', 'slab'))  63.7 us
    another operation x6, other arithmetic, solve_coeffs(): chol = jnp.linalg.cholesky(gram)  38.5 us
    add x1, other arithmetic, local(): new_velocity = velocity + section_gain * new_register  34.3 us
    reduce_sum x1, other arithmetic, coarsen(): field.reshape(comps, wide_x // 4, 4, wide_y // 4, 4, wide_z // 4, 4)  30.8 us
    slice x8, local copies, waits for them, and re-layouts, shift_y(): return jnp.roll(velocity, -offset, axis=2)  29.8 us
  transfers between devices with their start and end apart: 4, of which 1 were waited for; matrix products, arithmetic and copies ran while one was open for 24% of the time, Pallas kernels for 0%

commit v1 on v0

v1 whole, which is shorter than its diff:
```python
import functools

import jax
import jax.numpy as jnp
from jax import lax
from jax.experimental import pallas as pl
from jax.experimental.pallas import tpu as pltpu
from jax.sharding import PartitionSpec as P

first_coef = (0.8, -0.2, 4.0 / 105.0, -1.0 / 280.0)
second_coef = (-205.0 / 72.0, 1.6, -0.2, 8.0 / 315.0, -1.0 / 560.0)
time_step = 0.02
viscosity = 0.4
section_decay = -5.0 / 9.0
section_gain = 15.0 / 16.0
reach = 4

F32 = jnp.float32
BF16 = jnp.bfloat16
HIGH = lax.Precision.HIGHEST
NT = (((1,), (1,)), ((), ()))
TN = (((0,), (0,)), ((), ()))
NN = (((1,), (0,)), ((), ()))
N_GROUP = 8
N_SLAB = 16
RANK = 256
ROWS = 12288
COUNT = 8
PLANES = 4
LANES = 384
CHUNK = 1024
N_CHUNK = ROWS // CHUNK
BAND = RANK // N_SLAB
MIB = 2**20


def dot(left, right, dims, precision=None):
    return lax.dot_general(
        left, right, dims, precision=precision, preferred_element_type=F32
    )


def split(value):
    high = value.astype(BF16)
    return high, (value - high.astype(F32)).astype(BF16)


def peer(axis, step):
    group, slab = lax.axis_index("group"), lax.axis_index("slab")
    if axis == "group":
        return (lax.rem(group + step, N_GROUP), slab)
    return (group, lax.rem(slab + step, N_SLAB))


def linear(step):
    total = N_GROUP * N_SLAB
    place = lax.rem(lax.axis_index("group") * N_SLAB + lax.axis_index("slab") + step + total, total)
    return (place // N_SLAB, lax.rem(place, N_SLAB))


def greet(halo):
    barrier = pltpu.get_barrier_semaphore()
    count = 0
    for axis, size in (("group", N_GROUP), ("slab", N_SLAB)):

        def hello(step, carry, axis=axis):
            pl.semaphore_signal(barrier, inc=1, device_id=peer(axis, step))
            return carry

        lax.fori_loop(1, size, hello, 0)
        count += size - 1
    if halo:
        for step in (1, -1):
            pl.semaphore_signal(barrier, inc=1, device_id=linear(step))
            count += 1
    pl.semaphore_wait(barrier, count)


def broadcast(axis, size, source, target, send_sem, recv_sem):
    def send(step, carry):
        pltpu.make_async_remote_copy(
            src_ref=source(step),
            dst_ref=target,
            send_sem=send_sem,
            recv_sem=recv_sem,
            device_id=peer(axis, step),
        ).start()
        return carry

    lax.fori_loop(1, size, send, 0)


def drain(ref, *sems):
    for sem in sems:
        pltpu.make_async_copy(ref, ref, sem).wait()


def add_slots(ref):
    total = ref[0]
    for slot in range(1, ref.shape[0]):
        total = total + ref[slot]
    return total


def piece_of(owner, group):
    slab = lax.axis_index("slab")
    place = jnp.int32(0)
    for piece in range(N_GROUP):
        place = jnp.where(owner[slab, piece] == group, piece, place)
    return place


def front_kernel(
    velocity, basis, past, owner,
    low, high, gram, rows,
    field, edge_low, edge_high, blocks, past_v, pieces, ship, local, shares, partial, groups, band, full,
    field_sem, halo_send, halo_recv, block_sem, past_sem, piece_send, piece_recv, own_sem, sum_send, sum_recv, out_sem,
):
    group, slab = lax.axis_index("group"), lax.axis_index("slab")
    loads = [
        pltpu.make_async_copy(velocity.at[c], field.at[c], field_sem.at[c]) for c in range(3)
    ]
    for load in loads:
        load.start()
    past_load = pltpu.make_async_copy(past, past_v, past_sem)
    past_load.start()

    def block_load(step):
        lanes = pl.ds(pl.multiple_of(step * CHUNK, CHUNK), CHUNK)
        return pltpu.make_async_copy(basis.at[:, lanes], blocks.at[step], block_sem.at[step])

    def begin(step, carry):
        block_load(step).start()
        return carry

    lax.fori_loop(0, N_CHUNK, begin, 0)
    greet(True)

    halos = []
    for c in range(3):
        loads[c].wait()
        edge_low[c] = field[c, :, 0:reach, :]
        edge_high[c] = field[c, :, 16 - reach : 16, :]
        for side, (edge, target, step) in enumerate(((edge_high, low, 1), (edge_low, high, -1))):
            copy = pltpu.make_async_remote_copy(
                src_ref=edge.at[c],
                dst_ref=target.at[c],
                send_sem=halo_send.at[side, c],
                recv_sem=halo_recv.at[side, c],
                device_id=linear(step),
            )
            copy.start()
            halos.append(copy)

    past_load.wait()
    pieces[...] = jnp.zeros_like(pieces)

    def arrange(place, carry):
        piece, plane = place // PLANES, lax.rem(place, PLANES)
        parts = [past_v[:, plane, pl.ds(piece * 4 + j, 1), :].reshape(COUNT - 1, 96) for j in range(4)]
        pieces[piece, plane, 0 : COUNT - 1, :] = jnp.concatenate(parts, axis=1)
        return carry

    lax.fori_loop(0, N_GROUP * PLANES, arrange, 0)

    def pick(step, carry):
        ship[step] = pieces[piece_of(owner, lax.rem(group + step, N_GROUP))]
        return carry

    lax.fori_loop(0, N_GROUP, pick, 0)
    own = pltpu.make_async_copy(ship.at[0], rows.at[:, group], own_sem)
    own.start()
    broadcast("group", N_GROUP, lambda step: ship.at[step], rows.at[:, group], piece_send, piece_recv)

    local[...] = jnp.zeros_like(local)

    def multiply(step, carry):
        block_load(step).wait()
        top, rest = split(blocks[step])
        local[...] += dot(top, jnp.concatenate([top, rest], axis=0), NT)
        return carry

    lax.fori_loop(0, N_CHUNK, multiply, 0)
    cross = local[:, RANK:]
    partial[...] = (local[:, :RANK] + cross + cross.T).reshape(N_SLAB, BAND, RANK)

    broadcast(
        "slab", N_SLAB, lambda step: partial.at[lax.rem(slab + step, N_SLAB)], shares.at[slab],
        sum_send.at[0], sum_recv.at[0],
    )
    shares[slab] = partial[slab]
    drain(shares.at[pl.ds(0, N_SLAB - 1)], sum_recv.at[0], sum_send.at[0])
    groups[group] = add_slots(shares)
    broadcast(
        "group", N_GROUP, lambda step: groups.at[group], groups.at[group], sum_send.at[1], sum_recv.at[1]
    )
    drain(groups.at[pl.ds(0, N_GROUP - 1)], sum_recv.at[1], sum_send.at[1])
    band[...] = add_slots(groups) * (1.0 / (ROWS * N_GROUP * N_SLAB))
    full[slab] = band[...]
    broadcast("slab", N_SLAB, lambda step: band, full.at[slab], sum_send.at[2], sum_recv.at[2])
    drain(full.at[pl.ds(0, N_SLAB - 1)], sum_recv.at[2], sum_send.at[2])
    out = pltpu.make_async_copy(full, gram, out_sem)
    out.start()

    own.wait()
    drain(ship.at[pl.ds(0, N_GROUP - 1)], piece_recv, piece_send)
    for copy in halos:
        copy.wait()
    out.wait()


def front(velocity, basis, past, owner):
    any_space = pl.BlockSpec(memory_space=pl.ANY)
    return pl.pallas_call(
        front_kernel,
        in_specs=[any_space] * 3 + [pl.BlockSpec(memory_space=pltpu.SMEM)],
        out_specs=[any_space] * 4,
        out_shape=[
            jax.ShapeDtypeStruct((3, 128, reach, 128), F32),
            jax.ShapeDtypeStruct((3, 128, reach, 128), F32),
            jax.ShapeDtypeStruct((N_SLAB, BAND, RANK), F32),
            jax.ShapeDtypeStruct((PLANES, N_GROUP, COUNT, LANES), F32),
        ],
        scratch_shapes=[
            pltpu.VMEM((3, 128, 16, 128), F32),
            pltpu.VMEM((3, 128, reach, 128), F32),
            pltpu.VMEM((3, 128, reach, 128), F32),
            pltpu.VMEM((N_CHUNK, RANK, CHUNK), F32),
            pltpu.VMEM((COUNT - 1, PLANES, 32, 96), F32),
            pltpu.VMEM((N_GROUP, PLANES, COUNT, LANES), F32),
            pltpu.VMEM((N_GROUP, PLANES, COUNT, LANES), F32),
            pltpu.VMEM((RANK, 2 * RANK), F32),
            pltpu.VMEM((N_SLAB, BAND, RANK), F32),
            pltpu.VMEM((N_SLAB, BAND, RANK), F32),
            pltpu.VMEM((N_GROUP, BAND, RANK), F32),
            pltpu.VMEM((BAND, RANK), F32),
            pltpu.VMEM((N_SLAB, BAND, RANK), F32),
            pltpu.SemaphoreType.DMA((3,)),
            pltpu.SemaphoreType.DMA((2, 3)),
            pltpu.SemaphoreType.DMA((2, 3)),
            pltpu.SemaphoreType.DMA((N_CHUNK,)),
            pltpu.SemaphoreType.DMA,
            pltpu.SemaphoreType.DMA,
            pltpu.SemaphoreType.DMA,
            pltpu.SemaphoreType.DMA,
            pltpu.SemaphoreType.DMA((3,)),
            pltpu.SemaphoreType.DMA((3,)),
            pltpu.SemaphoreType.DMA,
        ],
        compiler_params=pltpu.CompilerParams(
            collective_id=0, has_side_effects=True, vmem_limit_bytes=56 * MIB
        ),
        name="front",
    )(velocity, basis, past, owner)


X_BLOCK = 16


def stencil_kernel(v, low, high, register, new_v, new_r, fresh, sums_ref):
    block = pl.program_id(0)

    def column(within):
        x = block * X_BLOCK + within
        center = [v[c, x] for c in range(3)]
        coef = []
        for axis in range(3):
            row = []
            for k in range(4):
                drift = center[axis] * first_coef[k]
                diffuse = viscosity * second_coef[k + 1]
                row.append((diffuse - drift, diffuse + drift))
            coef.append(row)
        outs = []
        for c in range(3):
            tall = jnp.concatenate([low[c, x], center[c], high[c, x]], axis=0)
            total = center[c] * (3.0 * viscosity * second_coef[0])
            for k in range(1, 5):
                up, down = coef[0][k - 1]
                total = total + v[c, (x + k) & 127] * up + v[c, (x - k) & 127] * down
            for k in range(1, 5):
                up, down = coef[1][k - 1]
                total = total + pltpu.roll(center[c], 128 - k, 1) * up
                total = total + pltpu.roll(center[c], k, 1) * down
            for k in range(1, 5):
                up, down = coef[2][k - 1]
                total = total + tall[reach + k : reach + k + 16] * up
                total = total + tall[reach - k : reach - k + 16] * down
            moved = register[c, within] * section_decay + time_step * total
            new_r[c, within] = moved
            fluid = center[c] + section_gain * moved
            new_v[c, within] = fluid
            outs.append(fluid)
        return outs

    def coarse(quad, carry):
        sums = column(quad * 4)
        for j in range(1, 4):
            sums = [a + b for a, b in zip(sums, column(quad * 4 + j))]
        across = block * (X_BLOCK // 4) + quad
        j, piece = across & 3, across >> 2
        for c in range(3):
            place = ((c * 4 + j) * N_GROUP + piece) * 16
            sums_ref[pl.ds(pl.multiple_of(place, 16), 16), :] = sums[c]
        return carry

    lax.fori_loop(0, X_BLOCK // 4, coarse, 0)

    @pl.when(block == pl.num_programs(0) - 1)
    def _():
        rows = sums_ref[pl.ds(0, 384, 4), :]
        for z in range(1, 4):
            rows = rows + sums_ref[pl.ds(z, 384, 4), :]
        row = lax.broadcasted_iota(jnp.int32, (512, 128), 0)
        lane = lax.broadcasted_iota(jnp.int32, (512, 128), 1)
        fold = jnp.where((row // 128 == lane // 32) & ((row % 128) // 4 == lane % 32), 1 / 64, 0.0)
        for tile in range(3):
            parts = []
            for m in range(4):
                j, c = divmod(4 * tile + m, 3)
                parts.append(rows[(c * 4 + j) * 32 : (c * 4 + j) * 32 + 32])
            fresh[:, tile * 128 : (tile + 1) * 128] = dot(
                jnp.concatenate(parts, axis=1), fold.astype(F32), NN, HIGH
            )


def stencil(velocity, low, high, register):
    vmem = pl.BlockSpec(memory_space=pltpu.VMEM)
    part = pl.BlockSpec((3, X_BLOCK, 16, 128), lambda i: (0, i, 0, 0))
    return pl.pallas_call(
        stencil_kernel,
        grid=(128 // X_BLOCK,),
        in_specs=[vmem, vmem, vmem, part],
        out_specs=[part, part, pl.BlockSpec((32, LANES), lambda i: (0, 0))],
        out_shape=[
            jax.ShapeDtypeStruct((3, 128, 16, 128), F32),
            jax.ShapeDtypeStruct((3, 128, 16, 128), F32),
            jax.ShapeDtypeStruct((32, LANES), F32),
        ],
        scratch_shapes=[pltpu.VMEM((1536, 128), F32)],
        compiler_params=pltpu.CompilerParams(vmem_limit_bytes=50 * MIB),
        name="stencil",
    )(velocity, low, high, register)


def sweep_block(block):
    size = block.shape[0]
    lane = lax.broadcasted_iota(jnp.int32, block.shape, 1)
    row = lax.broadcasted_iota(jnp.int32, block.shape, 0)
    for q in range(size):
        pivot = 1.0 / block[q : q + 1, q : q + 1]
        line = jnp.where(lane[:1] == q, -1.0, block[q : q + 1, :]) * pivot
        column = block[:, q : q + 1]
        block = jnp.where(lane == q, 0.0, block) - column * line
        block = jnp.where(row == q, line, block)
    return -block


BLOCK = 32


def invert(matrix):
    lane = lax.broadcasted_iota(jnp.int32, (BLOCK, RANK), 1)
    row = lax.broadcasted_iota(jnp.int32, (BLOCK, RANK), 0)
    wide = lax.broadcasted_iota(jnp.int32, (RANK, RANK), 1)
    for k in range(RANK // BLOCK):
        start = k * BLOCK
        panel = matrix[start : start + BLOCK, :]
        tile = start // 128 * 128
        diagonal = panel[:, tile : tile + 128]
        if start % 128:
            diagonal = pltpu.roll(diagonal, 128 - start % 128, 1)
        inverse = sweep_block(diagonal)[:, :BLOCK]
        inside = (lane >= start) & (lane < start + BLOCK)
        eye = jnp.where(lane - start == row, -1.0, 0.0)
        solved = dot(inverse, jnp.where(inside, eye, panel), NN, HIGH)
        inside = (wide >= start) & (wide < start + BLOCK)
        matrix[...] = jnp.where(inside, 0.0, matrix[...]) - dot(panel, solved, TN, HIGH)
        matrix[start : start + BLOCK, :] = solved


def back_kernel(
    rows, gram, basis, fresh, owner,
    coeffs, factor, directions,
    blocks, top, rest, rows_v, fresh_v, ship, pieces, sheet, matrix, proj_group, proj_slab, res_group, res_slab,
    block_sem, rows_sem, gram_sem, fresh_sem, piece_send, piece_recv, sum_send, sum_recv,
):
    group, slab = lax.axis_index("group"), lax.axis_index("slab")
    fresh_load = pltpu.make_async_copy(fresh, fresh_v, fresh_sem)
    fresh_load.start()
    gram_load = pltpu.make_async_copy(gram, matrix, gram_sem)
    gram_load.start()
    rows_load = pltpu.make_async_copy(rows, rows_v, rows_sem)
    rows_load.start()

    def block_load(step):
        lanes = pl.ds(pl.multiple_of(step * CHUNK, CHUNK), CHUNK)
        return pltpu.make_async_copy(basis.at[:, lanes], blocks.at[step], block_sem.at[step])

    def begin(step, carry):
        block_load(step).start()
        return carry

    lax.fori_loop(0, N_CHUNK, begin, 0)
    greet(False)
    fresh_load.wait()

    def pick(step, carry):
        ship[step] = fresh_v[piece_of(owner, lax.rem(group + step, N_GROUP))]
        return carry

    lax.fori_loop(0, N_GROUP, pick, 0)
    pieces[group] = ship[0]
    broadcast("group", N_GROUP, lambda step: ship.at[step], pieces.at[group], piece_send, piece_recv)

    gram_load.wait()
    invert(matrix)

    rows_load.wait()
    drain(pieces.at[pl.ds(0, N_GROUP - 1)], piece_recv, piece_send)
    last = lax.broadcasted_iota(jnp.int32, (COUNT, LANES), 0) == COUNT - 1
    for plane in range(PLANES):
        for h in range(N_GROUP):
            start = (plane * N_GROUP + h) * LANES
            sheet[:, start : start + LANES] = jnp.where(
                last, pieces[h, plane : plane + 1, :], rows_v[plane, h]
            )

    def lanes_of(step):
        return pl.ds(pl.multiple_of(step * CHUNK, CHUNK), CHUNK)

    def project(step, total):
        block_load(step).wait()
        upper, lower = split(blocks[step])
        top[step], rest[step] = upper, lower
        part = sheet[:, lanes_of(step)]
        head, tail = split(part)
        both = dot(jnp.concatenate([head, tail], axis=0), upper, NT)
        return total + both[:COUNT] + both[COUNT:] + dot(head, lower, NT)

    proj = lax.fori_loop(0, N_CHUNK, project, jnp.zeros((COUNT, RANK), F32))

    def sum_all(value, group_ref, slab_ref, place):
        group_ref[group] = value
        broadcast(
            "group", N_GROUP, lambda step: group_ref.at[group], group_ref.at[group],
            sum_send.at[place], sum_recv.at[place],
        )
        drain(group_ref.at[pl.ds(0, N_GROUP - 1)], sum_recv.at[place], sum_send.at[place])
        slab_ref[slab] = add_slots(group_ref)
        broadcast(
            "slab", N_SLAB, lambda step: slab_ref.at[slab], slab_ref.at[slab],
            sum_send.at[place + 1], sum_recv.at[place + 1],
        )
        drain(slab_ref.at[pl.ds(0, N_SLAB - 1)], sum_recv.at[place + 1], sum_send.at[place + 1])
        return add_slots(slab_ref) * (1.0 / (ROWS * N_GROUP * N_SLAB))

    proj = sum_all(proj, proj_group, proj_slab, 0)
    weights = -dot(proj, matrix[...], NN, HIGH)
    coeffs[...] = weights

    head, tail = split(weights)
    both_parts = jnp.concatenate([head, tail], axis=0)

    def subtract(step, total):
        both = dot(both_parts, top[step], NN)
        image = both[:COUNT] + both[COUNT:] + dot(head, rest[step], NN)
        part = sheet[:, lanes_of(step)] - image
        sheet[:, lanes_of(step)] = part
        return total + dot(part, part, NT, HIGH)

    wgram = lax.fori_loop(0, N_CHUNK, subtract, jnp.zeros((COUNT, COUNT), F32))
    wgram = jnp.concatenate([wgram, jnp.zeros((COUNT, 128 - COUNT), F32)], axis=1)
    wgram = sum_all(wgram, res_group, res_slab, 2)

    lane = lax.broadcasted_iota(jnp.int32, (COUNT, 128), 1)
    row = lax.broadcasted_iota(jnp.int32, (COUNT, 128), 0)
    lower = jnp.zeros((COUNT, 128), F32)
    inverse = jnp.where(lane == row, 1.0, 0.0)
    for q in range(COUNT):
        scale = lax.rsqrt(wgram[q : q + 1, q : q + 1])
        column = wgram[:, q : q + 1] * scale
        column = jnp.where(row[:, :1] >= q, column, 0.0)
        lower = jnp.where(lane == q, column, lower)
        line = wgram[q : q + 1, :] * scale
        below = jnp.where(row[:, :1] > q, column, 0.0)
        wgram = wgram - below * line
        solved = inverse[q : q + 1, :] * scale
        inverse = jnp.where(row == q, solved, inverse - below * solved)
    factor[...] = lower[:, :COUNT]
    columns = [inverse[:, q : q + 1] for q in range(COUNT)]

    def direct(step, carry):
        part = sheet[:, lanes_of(step)]
        total = columns[0] * part[0:1, :]
        for q in range(1, COUNT):
            total = total + columns[q] * part[q : q + 1, :]
        directions[:, lanes_of(step)] = total
        return carry

    lax.fori_loop(0, N_CHUNK, direct, 0)


def back(rows, gram, basis, fresh, owner):
    any_space = pl.BlockSpec(memory_space=pl.ANY)
    vmem = pl.BlockSpec(memory_space=pltpu.VMEM)
    return pl.pallas_call(
        back_kernel,
        in_specs=[any_space] * 4 + [pl.BlockSpec(memory_space=pltpu.SMEM)],
        out_specs=[vmem] * 3,
        out_shape=[
            jax.ShapeDtypeStruct((COUNT, RANK), F32),
            jax.ShapeDtypeStruct((COUNT, COUNT), F32),
            jax.ShapeDtypeStruct((COUNT, ROWS), F32),
        ],
        scratch_shapes=[
            pltpu.VMEM((N_CHUNK, RANK, CHUNK), F32),
            pltpu.VMEM((N_CHUNK, RANK, CHUNK), BF16),
            pltpu.VMEM((N_CHUNK, RANK, CHUNK), BF16),
            pltpu.VMEM((PLANES, N_GROUP, COUNT, LANES), F32),
            pltpu.VMEM((N_GROUP, PLANES, LANES), F32),
            pltpu.VMEM((N_GROUP, PLANES, LANES), F32),
            pltpu.VMEM((N_GROUP, PLANES, LANES), F32),
            pltpu.VMEM((COUNT, ROWS), F32),
            pltpu.VMEM((RANK, RANK), F32),
            pltpu.VMEM((N_GROUP, COUNT, RANK), F32),
            pltpu.VMEM((N_SLAB, COUNT, RANK), F32),
            pltpu.VMEM((N_GROUP, COUNT, 128), F32),
            pltpu.VMEM((N_SLAB, COUNT, 128), F32),
            pltpu.SemaphoreType.DMA((N_CHUNK,)),
            pltpu.SemaphoreType.DMA,
            pltpu.SemaphoreType.DMA,
            pltpu.SemaphoreType.DMA,
            pltpu.SemaphoreType.DMA,
            pltpu.SemaphoreType.DMA,
            pltpu.SemaphoreType.DMA((4,)),
            pltpu.SemaphoreType.DMA((4,)),
        ],
        compiler_params=pltpu.CompilerParams(
            collective_id=1, has_side_effects=True, vmem_limit_bytes=56 * MIB
        ),
        name="back",
    )(rows, gram, basis, fresh, owner)


def local(velocity, register, past, basis, owner):
    field = velocity.transpose(0, 1, 3, 2)
    blocks = basis.reshape(RANK, ROWS)
    low, high, gram, rows = front(field, blocks, past, owner)
    new_v, new_r, fresh = stencil(field, low, high, register.transpose(0, 1, 3, 2))
    coeffs, factor, directions = back(
        rows, gram.reshape(RANK, RANK), blocks, fresh.reshape(N_GROUP, PLANES, LANES), owner
    )
    return (
        new_v.transpose(0, 1, 3, 2),
        new_r.transpose(0, 1, 3, 2),
        coeffs.T,
        factor,
        directions.reshape(1, 1, COUNT, ROWS),
    )


def solution(mesh):
    in_specs = (
        P(None, None, None, ("group", "slab")),
        P(None, None, None, ("group", "slab")),
        P(None, ("group", "slab"), None, None),
        P("slab", "group", None, None),
        P(),
    )
    out_specs = (
        P(None, None, None, ("group", "slab")),
        P(None, None, None, ("group", "slab")),
        P(),
        P(),
        P("slab", "group", None, None),
    )
    return jax.shard_map(local, mesh=mesh, in_specs=in_specs, out_specs=out_specs, check_vma=False)
```

time: 600 us -> 132 us (0.22)
  local copies, waits for them, and re-layouts: 176 us -> 8.59 us
  other arithmetic: 132 us -> 0 us
  blocking collectives: 129 us -> 0 us
  Pallas kernels: 0 us -> 122 us
  waiting for transfers between devices: 93 us -> 0 us
  matrix products: 43.1 us -> 0 us
  between operations: 15.8 us -> 0.66 us
  starting transfers between devices: 7.35 us -> 0 us
    psum x2 -> x0, blocking collectives: 129 us -> none  [the longest x1 65.6 us: local(): proj, gram = lax.psum((proj_local, gram_local), ('group', 'slab'))]
    pallas_call x0 -> x3, Pallas kernels: none -> 122 us  [the longest x1 61.8 us: back(): pl.pallas_call(back_kernel, in_specs=[any_space] * 4 + [pl.BlockSpec(memo...]
    reshape x2 -> x1, local copies, waits for them, and re-layouts: 107 us -> 0.64 us  [local(): fresh.reshape(N_GROUP, PLANES, LANES)]
    psum x1 -> x0, waiting for transfers between devices: 93 us -> none  [local(): proj, gram = lax.psum((proj_local, gram_local), ('group', 'slab'))]
    another operation x15 -> x0, other arithmetic: 63.4 us -> none  [the longest x6 38.5 us: solve_coeffs(): chol = jnp.linalg.cholesky(gram)]
    slice x17 -> x0, local copies, waits for them, and re-layouts: 47.1 us -> none  [the longest x8 29.8 us: shift_y(): return jnp.roll(velocity, -offset, axis=2)]
    dot_general x4 -> x0, matrix products: 37.9 us -> none  [the longest x3 28.9 us: inner(): lax.dot_general(left, right, (((1,), (1,)), ((), ())), precision=lax.Prec...]
    add x1 -> x0, other arithmetic: 34.3 us -> none  [local(): new_velocity = velocity + section_gain * new_register]
  transfers between devices with their start and end apart: 4 -> 0, of which waited for: 1 -> 0; matrix products, arithmetic and copies ran while one was open for 24% -> 0% of each run, Pallas kernels for 0% -> 0%
where the time goes in v1:
time: 132 us
  Pallas kernels  122 us (92%)
  local copies, waits for them, and re-layouts  8.59 us (7%)
    pallas_call x1, Pallas kernels, back(): pl.pallas_call(back_kernel, in_specs=[any_space] * 4 + [pl.BlockSpec(memo...  61.8 us
    pallas_call x1, Pallas kernels, front(): pl.pallas_call(front_kernel, in_specs=[any_space] * 3 + [pl.BlockSpec(mem...  46.5 us
    pallas_call x1, Pallas kernels, stencil(): pl.pallas_call(stencil_kernel, grid=(128 // X_BLOCK,), in_specs=[vmem, vm...  14.3 us
    unnamed x8, local copies, waits for them, and re-layouts  7.95 us

profile of v1, /device:TPU:1, one launch (start us, length us, event | category | flops | bytes accessed | tf_op | source)
XLA Modules:
  0.0 131.7 jit_solution(3495431744782224196)
XLA Ops:
  0.6 1.4 %copy.10.owner = s32[16,8]{1,0:T(8,128)} copy(s32[16,8]{0,1:T(8,128)} %param.9) | data formatting | bytes 1024 | tf_op args[4]
  2.0 46.5 %front.1 = (f32[3,128,4,128]{3,2,1,0:T(4,128)}, f32[3,128,4,128]{3,2,1,0:T(4,128)}, f32[16,16,256]{2,1,0:T(8,128)}, f32[4,8,8,384]{3,2,1,0:T(8,128)}) custom-call(f32[3,128,16,128]{3,2,1,0:T(8,128)} %bitcast.10, f32[256,12288]{1,0:T(8,128)} %bitcast.8, f32[7,4,32,96]{3,2,1,0:T(8,128)} %past.1, s32[16,8]{1,0:T(8,128)} %copy.10.owner), custom_call_target="tpu_custom_call" | custom-call | tf_op jit(solution)/shard_map/front/pallas_call | solution.py:214
  48.4 0.0 copy-start
  48.5 1.1 copy-done
  49.6 0.0 copy-start.1
  49.6 1.1 copy-done.1
  50.7 14.3 %stencil.1 = (f32[3,128,16,128]{3,2,1,0:T(8,128)}, f32[3,128,16,128]{3,2,1,0:T(8,128)}, f32[32,384]{1,0:T(8,128)S(1)}) custom-call(f32[3,128,16,128]{3,2,1,0:T(8,128)} %bitcast.11, f32[3,128,4,128]{3,2,1,0:T(4,128)S(1)} %copy-done, f32[3,128,4,128]{3,2,1,0:T(4,128)S(1)} %copy-done.1, f32[3,128,16,128]{3,2,1,0:T(8,128)} %bitcast.12), custom_call_target="tpu_custom_call" | custom-call | tf_op jit(solution)/shard_map/stencil/pallas_call | solution.py:330
  65.0 0.6 reshape.24.fresh
  65.6 61.8 %back.1 = (f32[8,256]{1,0:T(8,128)}, f32[8,8]{1,0:T(8,128)}, f32[8,12288]{1,0:T(8,128)}) custom-call(f32[4,8,8,384]{3,2,1,0:T(8,128)} %get-tuple-element.19.rows, f32[256,256]{1,0:T(8,128)} %bitcast.14, f32[256,12288]{1,0:T(8,128)} %bitcast.9, f32[8,4,384]{2,1,0:T(4,128)} %reshape.24.fresh, s32[16,8]{1,0:T(8,128)} %copy.10.owner), custom_call_target="tpu_custom_call" | custom-call | tf_op jit(solution)/shard_map/back/pallas_call | solution.py:507
  127.4 1.3 copy.15
  128.7 1.3 copy.16
  130.0 1.8 %copy.17 = f32[1,1,8,12288]{3,2,1,0:T(8,128)} copy(f32[1,1,8,12288]{3,2,1,0:T(8,128)} %bitcast.13) | data formatting | bytes 786432
Async XLA Ops:
  48.4 1.1 copy-start
  49.6 1.1 copy-start.1

commit v2 on v0

v2 whole, which is shorter than its diff:
```python
import functools

import jax
import jax.numpy as jnp
from jax import lax
from jax.experimental import pallas as pl
from jax.experimental.pallas import tpu as pltpu
from jax.sharding import PartitionSpec as P

first_coef = (0.8, -0.2, 4.0 / 105.0, -1.0 / 280.0)
second_coef = (-205.0 / 72.0, 1.6, -0.2, 8.0 / 315.0, -1.0 / 560.0)
time_step = 0.02
viscosity = 0.4
section_decay = -5.0 / 9.0
section_gain = 15.0 / 16.0
reach = 4

F32 = jnp.float32
BF16 = jnp.bfloat16
HIGH = lax.Precision.HIGHEST
NT = (((1,), (1,)), ((), ()))
TN = (((0,), (0,)), ((), ()))
NN = (((1,), (0,)), ((), ()))
N_GROUP = 8
N_SLAB = 16
N_POLE = 8
N_PLANE = 16
RANK = 256
ROWS = 12288
COUNT = 8
PLANES = 4
LANES = 384
CHUNK = 1024
N_CHUNK = ROWS // CHUNK
BAND = RANK // N_SLAB
X_CHUNK = 16
N_X = 128 // X_CHUNK
BLOCK = 32
MIB = 2**20


def dot(left, right, dims, precision=None):
    return lax.dot_general(
        left, right, dims, precision=precision, preferred_element_type=F32
    )


def split(value):
    high = value.astype(BF16)
    return high, (value - high.astype(F32)).astype(BF16)


def peer(axis, step):
    group, slab = lax.axis_index("group"), lax.axis_index("slab")
    if axis == "group":
        return (lax.rem(group + step, N_GROUP), slab)
    if axis == "slab":
        return (group, lax.rem(slab + step, N_SLAB))
    column = lax.rem(slab // 2, 2)
    if axis == "pole":
        place = lax.rem(pole_index() + step, N_POLE)
        return (group, place // 2 * 4 + column * 2 + lax.rem(place, 2))
    place = lax.rem(plane_index() + step, N_PLANE)
    return (place // 2, slab - column * 2 + lax.rem(place, 2) * 2)


def pole_index():
    slab = lax.axis_index("slab")
    return slab // 4 * 2 + lax.rem(slab, 2)


def plane_index():
    return lax.axis_index("group") * 2 + lax.rem(lax.axis_index("slab") // 2, 2)


def linear(step):
    total = N_GROUP * N_SLAB
    place = lax.rem(lax.axis_index("group") * N_SLAB + lax.axis_index("slab") + step + total, total)
    return (place // N_SLAB, lax.rem(place, N_SLAB))


def hello():
    barrier = pltpu.get_barrier_semaphore()
    for axis, size in (("slab", N_SLAB), ("plane", N_PLANE)):

        def signal(step, carry, axis=axis):
            pl.semaphore_signal(barrier, inc=1, device_id=peer(axis, step))
            return carry

        lax.fori_loop(1, size, signal, 0)
    for step in (1, -1):
        pl.semaphore_signal(barrier, inc=1, device_id=linear(step))


def everyone_in():
    pl.semaphore_wait(pltpu.get_barrier_semaphore(), N_SLAB + N_PLANE)


def broadcast(axis, size, source, target, send_sem, recv_sem):
    def send(step, carry):
        pltpu.make_async_remote_copy(
            src_ref=source(step),
            dst_ref=target,
            send_sem=send_sem,
            recv_sem=recv_sem,
            device_id=peer(axis, step),
        ).start()
        return carry

    lax.fori_loop(1, size, send, 0)


def drain(ref, *sems):
    for sem in sems:
        pltpu.make_async_copy(ref, ref, sem).wait()


def add_slots(ref):
    total = ref[0]
    for slot in range(1, ref.shape[0]):
        total = total + ref[slot]
    return total


def piece_of(owner, group):
    slab = lax.axis_index("slab")
    place = jnp.int32(0)
    for piece in range(N_GROUP):
        place = jnp.where(owner[piece, slab] == group, piece, place)
    return place


def sweep_block(block):
    lane = lax.broadcasted_iota(jnp.int32, (8, 128), 1)
    row = lax.broadcasted_iota(jnp.int32, (8, 128), 0)
    count = block.shape[0] // 8
    parts = [block[8 * i : 8 * i + 8] for i in range(count)]
    for b in range(count):
        line = parts[b]
        columns = [jnp.broadcast_to(line[:, 8 * b + j : 8 * b + j + 1], (8, 128)) for j in range(8)]
        inside = (lane >= 8 * b) & (lane < 8 * b + 8)
        line = jnp.where(inside, jnp.where(lane - 8 * b == row, -1.0, 0.0), line)
        for q in range(8):
            pivot = 1.0 / columns[q][q : q + 1, :]
            solved = line[q : q + 1, :] * pivot
            others = jnp.where(row == q, 0.0, columns[q])
            line = jnp.where(row == q, solved, line - others * solved)
            for j in range(q + 1, 8):
                entry = columns[j][q : q + 1, :] * pivot
                columns[j] = jnp.where(row == q, entry, columns[j] - others * entry)
        for i in range(count):
            if i != b:
                part = parts[i]
                total = jnp.where(inside, 0.0, part)
                for j in range(8):
                    column = jnp.broadcast_to(part[:, 8 * b + j : 8 * b + j + 1], (8, 128))
                    total = total - column * line[j : j + 1, :]
                parts[i] = total
        parts[b] = line
    return -jnp.concatenate(parts, axis=0)


def invert(matrix, first, last):
    lane = lax.broadcasted_iota(jnp.int32, (BLOCK, RANK), 1)
    row = lax.broadcasted_iota(jnp.int32, (BLOCK, RANK), 0)
    wide = lax.broadcasted_iota(jnp.int32, (RANK, RANK), 1)
    for k in range(first, last):
        start = k * BLOCK
        panel = matrix[start : start + BLOCK, :]
        tile = start // 128 * 128
        diagonal = panel[:, tile : tile + 128]
        if start % 128:
            diagonal = pltpu.roll(diagonal, 128 - start % 128, 1)
        inverse = sweep_block(diagonal)[:, :BLOCK]
        inside = (lane >= start) & (lane < start + BLOCK)
        eye = jnp.where(lane - start == row, -1.0, 0.0)
        solved = dot(inverse, jnp.where(inside, eye, panel), NN, HIGH)
        inside = (wide >= start) & (wide < start + BLOCK)
        matrix[...] = jnp.where(inside, 0.0, matrix[...]) - dot(panel, solved, TN, HIGH)
        matrix[start : start + BLOCK, :] = solved


def fold_fresh(sums_ref, fresh):
    rows = sums_ref[pl.ds(0, 384, 4), :]
    for z in range(1, 4):
        rows = rows + sums_ref[pl.ds(z, 384, 4), :]
    row = lax.broadcasted_iota(jnp.int32, (512, 128), 0)
    lane = lax.broadcasted_iota(jnp.int32, (512, 128), 1)
    fold = jnp.where((row // 128 == lane // 32) & ((row % 128) // 4 == lane % 32), 1 / 64, 0.0)
    for tile in range(3):
        parts = []
        for m in range(4):
            j, c = divmod(4 * tile + m, 3)
            parts.append(rows[(c * 4 + j) * 32 : (c * 4 + j) * 32 + 32])
        part = dot(jnp.concatenate(parts, axis=1), fold.astype(F32), NN, HIGH)
        fresh[:, :, tile * 128 : (tile + 1) * 128] = part.reshape(N_GROUP, PLANES, 128)


def column(v, low, high, register, new_v, x):
    center = [v[c, x] for c in range(3)]
    coef = []
    for axis in range(3):
        row = []
        for k in range(4):
            drift = center[axis] * first_coef[k]
            diffuse = viscosity * second_coef[k + 1]
            row.append((diffuse - drift, diffuse + drift))
        coef.append(row)
    outs = []
    for c in range(3):
        tall = jnp.concatenate([low[c, x], center[c], high[c, x]], axis=0)
        total = center[c] * (3.0 * viscosity * second_coef[0])
        for k in range(1, 5):
            up, down = coef[0][k - 1]
            total = total + v[c, (x + k) & 127] * up + v[c, (x - k) & 127] * down
        for k in range(1, 5):
            up, down = coef[1][k - 1]
            total = total + pltpu.roll(center[c], 128 - k, 1) * up
            total = total + pltpu.roll(center[c], k, 1) * down
        for k in range(1, 5):
            up, down = coef[2][k - 1]
            total = total + tall[reach + k : reach + k + 16] * up
            total = total + tall[reach - k : reach - k + 16] * down
        moved = register[c, x] * section_decay + time_step * total
        register[c, x] = moved
        fluid = center[c] + section_gain * moved
        new_v[c, x] = fluid
        outs.append(fluid)
    return outs


def section_kernel(
    velocity, register, basis, past, owner,
    out_v, out_r, weights, wgram, sheet,
    field, reg, new_v, edge_low, edge_high, low, high, blocks, top, rest, past_v, pieces, ship, rows,
    local, partial, shares, groups, band, full, matrix, sums_ref, fresh, fresh_ship, fresh_in,
    proj_pole, proj_plane, res_pole, res_plane,
    field_sem, reg_sem, halo_send, halo_recv, block_sem, past_sem, piece_send, piece_recv, sum_send, sum_recv,
    out_sem,
):
    group, slab = lax.axis_index("group"), lax.axis_index("slab")
    hello()

    def part_of(chunk):
        return pl.ds(pl.multiple_of(chunk * X_CHUNK, X_CHUNK), X_CHUNK)

    def lanes_of(step):
        return pl.ds(pl.multiple_of(step * CHUNK, CHUNK), CHUNK)

    def field_load(chunk):
        part = part_of(chunk)
        return pltpu.make_async_copy(velocity.at[:, part], field.at[:, part], field_sem.at[chunk])

    def reg_load(chunk):
        part = part_of(chunk)
        return pltpu.make_async_copy(register.at[:, part], reg.at[:, part], reg_sem.at[chunk])

    def block_load(step):
        return pltpu.make_async_copy(basis.at[:, lanes_of(step)], blocks.at[step], block_sem.at[step])

    def start_each(count, make):
        def begin(step, carry):
            make(step).start()
            return carry

        lax.fori_loop(0, count, begin, 0)

    start_each(N_X, field_load)
    past_load = pltpu.make_async_copy(past, past_v, past_sem)
    past_load.start()
    start_each(N_CHUNK, block_load)
    start_each(N_X, reg_load)

    def halo(chunk, side):
        part = part_of(chunk)
        edge, target = ((edge_high, low), (edge_low, high))[side]
        return pltpu.make_async_remote_copy(
            src_ref=edge.at[:, part],
            dst_ref=target.at[:, part],
            send_sem=halo_send.at[side, chunk],
            recv_sem=halo_recv.at[side, chunk],
            device_id=linear((1, -1)[side]),
        )

    def face(chunk, carry):
        field_load(chunk).wait()
        part = part_of(chunk)
        edge_low[:, part] = field[:, part, 0:reach, :]
        edge_high[:, part] = field[:, part, 16 - reach : 16, :]
        return carry

    def face_send(chunk, carry):
        halo(chunk, 0).start()
        halo(chunk, 1).start()
        return carry

    lax.fori_loop(0, N_X, face, 0)
    everyone_in()
    lax.fori_loop(0, N_X, face_send, 0)

    past_load.wait()
    pieces[...] = jnp.zeros_like(pieces)

    def arrange(place, carry):
        piece, plane = place // PLANES, lax.rem(place, PLANES)
        parts = [past_v[:, plane, pl.ds(piece * 4 + j, 1), :].reshape(COUNT - 1, 96) for j in range(4)]
        pieces[piece, plane, 0 : COUNT - 1, :] = jnp.concatenate(parts, axis=1)
        return carry

    lax.fori_loop(0, N_GROUP * PLANES, arrange, 0)

    def pick(step, carry):
        ship[step] = pieces[piece_of(owner, lax.rem(group + step, N_GROUP))]
        return carry

    lax.fori_loop(0, N_GROUP, pick, 0)
    rows[:, group] = ship[0]
    broadcast(
        "group", N_GROUP, lambda step: ship.at[step], rows.at[:, group], piece_send.at[0], piece_recv.at[0]
    )

    local[...] = jnp.zeros_like(local)

    def multiply(step, carry):
        block_load(step).wait()
        upper, lower = split(blocks[step])
        top[step], rest[step] = upper, lower
        local[...] += dot(upper, jnp.concatenate([upper, lower], axis=0), NT)
        return carry

    lax.fori_loop(0, N_CHUNK, multiply, 0)
    cross = local[:, RANK:]
    partial[...] = (local[:, :RANK] + cross + cross.T).reshape(N_SLAB, BAND, RANK)

    def gram_first():
        broadcast(
            "slab", N_SLAB, lambda step: partial.at[lax.rem(slab + step, N_SLAB)], shares.at[slab],
            sum_send.at[0], sum_recv.at[0],
        )
        shares[slab] = partial[slab]

    def gram_second():
        drain(shares.at[pl.ds(0, N_SLAB - 1)], sum_recv.at[0])
        groups[group] = add_slots(shares)
        broadcast(
            "group", N_GROUP, lambda step: groups.at[group], groups.at[group], sum_send.at[1], sum_recv.at[1]
        )

    def gram_third():
        drain(groups.at[pl.ds(0, N_GROUP - 1)], sum_recv.at[1])
        band[...] = add_slots(groups) * (1.0 / (ROWS * N_GROUP * N_SLAB))
        full[slab] = band[...]
        broadcast("slab", N_SLAB, lambda step: band, full.at[slab], sum_send.at[2], sum_recv.at[2])

    def out_copy(chunk, which):
        part = part_of(chunk)
        source, target = ((new_v, out_v), (reg, out_r))[which]
        return pltpu.make_async_copy(source.at[:, part], target.at[:, part], out_sem.at[which, chunk])

    def stencil(chunk, carry):
        halo(chunk, 0).wait_recv()
        halo(chunk, 1).wait_recv()
        reg_load(chunk).wait()

        def coarse(quad, carry):
            x = chunk * X_CHUNK + quad * 4
            sums = column(field, low, high, reg, new_v, x)
            for j in range(1, 4):
                sums = [a + b for a, b in zip(sums, column(field, low, high, reg, new_v, x + j))]
            across = chunk * (X_CHUNK // 4) + quad
            j, piece = lax.rem(across, 4), across // 4
            for c in range(3):
                place = ((c * 4 + j) * N_GROUP + piece) * 16
                sums_ref[pl.ds(pl.multiple_of(place, 16), 16), :] = sums[c]
            return carry

        lax.fori_loop(0, X_CHUNK // 4, coarse, 0)
        out_copy(chunk, 0).start()
        out_copy(chunk, 1).start()
        return carry

    gram_first()
    lax.fori_loop(0, SECOND_AT, stencil, 0)
    gram_second()
    lax.fori_loop(SECOND_AT, THIRD_AT, stencil, 0)
    gram_third()
    lax.fori_loop(THIRD_AT, N_X, stencil, 0)

    fold_fresh(sums_ref, fresh)

    def pick_fresh(step, carry):
        fresh_ship[step] = fresh[piece_of(owner, lax.rem(group + step, N_GROUP))]
        return carry

    lax.fori_loop(0, N_GROUP, pick_fresh, 0)
    fresh_in[group] = fresh_ship[0]
    broadcast(
        "group", N_GROUP, lambda step: fresh_ship.at[step], fresh_in.at[group], piece_send.at[1], piece_recv.at[1]
    )

    drain(full.at[pl.ds(0, N_SLAB - 1)], sum_recv.at[2])
    matrix[...] = full[...].reshape(RANK, RANK)
    invert(matrix, 0, 2)

    drain(ship.at[pl.ds(0, N_GROUP - 1)], piece_recv.at[0])
    drain(fresh_ship.at[pl.ds(0, N_GROUP - 1)], piece_recv.at[1])
    last = lax.broadcasted_iota(jnp.int32, (COUNT, LANES), 0) == COUNT - 1
    for plane in range(PLANES):
        for h in range(N_GROUP):
            start = (plane * N_GROUP + h) * LANES
            sheet[:, start : start + LANES] = jnp.where(
                last, fresh_in[h, plane : plane + 1, :], rows[plane, h]
            )

    def project(step, total):
        head, tail = split(sheet[:, lanes_of(step)])
        both = dot(jnp.concatenate([head, tail], axis=0), top[step], NT)
        return total + both[:COUNT] + both[COUNT:] + dot(head, rest[step], NT)

    proj = lax.fori_loop(0, N_CHUNK, project, jnp.zeros((COUNT, RANK), F32))

    def sum_first(value, pole_ref, place):
        pole = pole_index()
        pole_ref[pole] = value
        broadcast(
            "pole", N_POLE, lambda step: pole_ref.at[pole], pole_ref.at[pole],
            sum_send.at[place], sum_recv.at[place],
        )

    def sum_second(pole_ref, plane_ref, place):
        drain(pole_ref.at[pl.ds(0, N_POLE - 1)], sum_recv.at[place])
        plane = plane_index()
        plane_ref[plane] = add_slots(pole_ref)
        broadcast(
            "plane", N_PLANE, lambda step: plane_ref.at[plane], plane_ref.at[plane],
            sum_send.at[place + 1], sum_recv.at[place + 1],
        )

    def sum_end(plane_ref, place):
        drain(plane_ref.at[pl.ds(0, N_PLANE - 1)], sum_recv.at[place + 1])
        return add_slots(plane_ref) * (1.0 / (ROWS * N_GROUP * N_SLAB))

    sum_first(proj, proj_pole, 3)
    invert(matrix, 2, 4)
    sum_second(proj_pole, proj_plane, 3)
    invert(matrix, 4, RANK // BLOCK)
    proj = sum_end(proj_plane, 3)
    solved = -dot(proj, matrix[...], NN, HIGH)
    weights[...] = solved

    head, tail = split(solved)
    both_parts = jnp.concatenate([head, tail], axis=0)

    def subtract(step, total):
        both = dot(both_parts, top[step], NN)
        image = both[:COUNT] + both[COUNT:] + dot(head, rest[step], NN)
        part = sheet[:, lanes_of(step)] - image
        sheet[:, lanes_of(step)] = part
        return total + dot(part, part, NT, HIGH)

    inner = lax.fori_loop(0, N_CHUNK, subtract, jnp.zeros((COUNT, COUNT), F32))
    sum_first(jnp.concatenate([inner, jnp.zeros((COUNT, 128 - COUNT), F32)], axis=1), res_pole, 5)

    def finish(chunk, carry):
        for which in range(2):
            halo(chunk, which).wait_send()
            out_copy(chunk, which).wait()
        return carry

    lax.fori_loop(0, N_X, finish, 0)
    drain(ship.at[pl.ds(0, N_GROUP - 1)], piece_send.at[0])
    drain(fresh_ship.at[pl.ds(0, N_GROUP - 1)], piece_send.at[1])
    drain(shares.at[pl.ds(0, N_SLAB - 1)], sum_send.at[0])
    drain(groups.at[pl.ds(0, N_GROUP - 1)], sum_send.at[1])
    drain(full.at[pl.ds(0, N_SLAB - 1)], sum_send.at[2])
    drain(proj_pole.at[pl.ds(0, N_POLE - 1)], sum_send.at[3])
    drain(proj_plane.at[pl.ds(0, N_PLANE - 1)], sum_send.at[4])
    sum_second(res_pole, res_plane, 5)
    drain(res_pole.at[pl.ds(0, N_POLE - 1)], sum_send.at[5])
    wgram[...] = sum_end(res_plane, 5)
    drain(res_plane.at[pl.ds(0, N_PLANE - 1)], sum_send.at[6])


SECOND_AT = 4
THIRD_AT = 8


def section(velocity, register, basis, past, owner):
    any_space = pl.BlockSpec(memory_space=pl.ANY)
    vmem = pl.BlockSpec(memory_space=pltpu.VMEM)
    dma = pltpu.SemaphoreType.DMA
    field = (3, 128, 16, 128)
    face = (3, 128, reach, 128)
    pieces = (N_GROUP, PLANES, COUNT, LANES)
    fresh = (N_GROUP, PLANES, LANES)
    scratch = [
        (field, F32), (field, F32), (field, F32), (face, F32), (face, F32), (face, F32), (face, F32),
        ((N_CHUNK, RANK, CHUNK), F32), ((N_CHUNK, RANK, CHUNK), BF16), ((N_CHUNK, RANK, CHUNK), BF16),
        ((COUNT - 1, PLANES, 32, 96), F32), (pieces, F32), (pieces, F32), ((PLANES, N_GROUP, COUNT, LANES), F32),
        ((RANK, 2 * RANK), F32), ((N_SLAB, BAND, RANK), F32), ((N_SLAB, BAND, RANK), F32),
        ((N_GROUP, BAND, RANK), F32), ((BAND, RANK), F32), ((N_SLAB, BAND, RANK), F32), ((RANK, RANK), F32),
        ((1536, 128), F32), (fresh, F32), (fresh, F32), (fresh, F32),
        ((N_POLE, COUNT, RANK), F32), ((N_PLANE, COUNT, RANK), F32),
        ((N_POLE, COUNT, 128), F32), ((N_PLANE, COUNT, 128), F32),
    ]
    semaphores = [(N_X,), (N_X,), (2, N_X), (2, N_X), (N_CHUNK,), None, (2,), (2,), (7,), (7,), (2, N_X)]
    return pl.pallas_call(
        section_kernel,
        in_specs=[any_space] * 4 + [pl.BlockSpec(memory_space=pltpu.SMEM)],
        out_specs=[any_space] * 2 + [vmem] * 3,
        out_shape=[
            jax.ShapeDtypeStruct(field, F32),
            jax.ShapeDtypeStruct(field, F32),
            jax.ShapeDtypeStruct((COUNT, RANK), F32),
            jax.ShapeDtypeStruct((COUNT, 128), F32),
            jax.ShapeDtypeStruct((COUNT, ROWS), F32),
        ],
        scratch_shapes=[pltpu.VMEM(shape, kind) for shape, kind in scratch]
        + [dma if shape is None else dma(shape) for shape in semaphores],
        compiler_params=pltpu.CompilerParams(
            collective_id=0, has_side_effects=True, vmem_limit_bytes=58 * MIB
        ),
        name="section",
    )(velocity, register, basis, past, owner)


def finish_kernel(weights, wgram_ref, residual, coeffs, factor, directions):
    coeffs[...] = weights[...]
    wgram = wgram_ref[...]
    lane = lax.broadcasted_iota(jnp.int32, (COUNT, 128), 1)
    row = lax.broadcasted_iota(jnp.int32, (COUNT, 128), 0)
    lower = jnp.zeros((COUNT, 128), F32)
    inverse = jnp.where(lane == row, 1.0, 0.0)
    for q in range(COUNT):
        scale = lax.rsqrt(wgram[q : q + 1, q : q + 1])
        column = wgram[:, q : q + 1] * scale
        column = jnp.where(row[:, :1] >= q, column, 0.0)
        lower = jnp.where(lane == q, column, lower)
        line = wgram[q : q + 1, :] * scale
        below = jnp.where(row[:, :1] > q, column, 0.0)
        wgram = wgram - below * line
        solved = inverse[q : q + 1, :] * scale
        inverse = jnp.where(row == q, solved, inverse - below * solved)
    factor[...] = lower[:, :COUNT]
    columns = [inverse[:, q : q + 1] for q in range(COUNT)]

    def direct(step, carry):
        lanes = pl.ds(pl.multiple_of(step * CHUNK, CHUNK), CHUNK)
        part = residual[:, lanes]
        total = columns[0] * part[0:1, :]
        for q in range(1, COUNT):
            total = total + columns[q] * part[q : q + 1, :]
        directions[:, lanes] = total
        return carry

    lax.fori_loop(0, N_CHUNK, direct, 0)


def finish(weights, wgram, residual):
    return pl.pallas_call(
        finish_kernel,
        out_shape=[
            jax.ShapeDtypeStruct((COUNT, RANK), F32),
            jax.ShapeDtypeStruct((COUNT, COUNT), F32),
            jax.ShapeDtypeStruct((COUNT, ROWS), F32),
        ],
        name="finish",
    )(weights, wgram, residual)


def local(velocity, register, past, basis, owner):
    new_v, new_r, weights, wgram, residual = section(
        velocity.transpose(0, 1, 3, 2), register.transpose(0, 1, 3, 2), basis.reshape(RANK, ROWS), past, owner.T
    )
    coeffs, factor, directions = finish(weights, wgram, residual)
    return (
        new_v.transpose(0, 1, 3, 2),
        new_r.transpose(0, 1, 3, 2),
        coeffs.T,
        factor,
        directions.reshape(1, 1, COUNT, ROWS),
    )


def solution(mesh):
    in_specs = (
        P(None, None, None, ("group", "slab")),
        P(None, None, None, ("group", "slab")),
        P(None, ("group", "slab"), None, None),
        P("slab", "group", None, None),
        P(),
    )
    out_specs = (
        P(None, None, None, ("group", "slab")),
        P(None, None, None, ("group", "slab")),
        P(),
        P(),
        P("slab", "group", None, None),
    )
    return jax.shard_map(local, mesh=mesh, in_specs=in_specs, out_specs=out_specs, check_vma=False)
```

time: 600 us -> 88.7 us (0.15)
  local copies, waits for them, and re-layouts: 176 us -> 5.58 us
  other arithmetic: 132 us -> 0 us
  blocking collectives: 129 us -> 0 us
  waiting for transfers between devices: 93 us -> 0 us
  Pallas kernels: 0 us -> 82.3 us
  matrix products: 43.1 us -> 0 us
  between operations: 15.8 us -> 0.64 us
  starting transfers between devices: 7.35 us -> 0 us
    psum x2 -> x0, blocking collectives: 129 us -> none  [the longest x1 65.6 us: local(): proj, gram = lax.psum((proj_local, gram_local), ('group', 'slab'))]
    reshape x2 -> x0, local copies, waits for them, and re-layouts: 107 us -> none  [the longest x1 106 us: coarsen(): field.reshape(comps, wide_x // 4, 4, wide_y // 4, 4, wide_z // 4, 4)]
    psum x1 -> x0, waiting for transfers between devices: 93 us -> none  [local(): proj, gram = lax.psum((proj_local, gram_local), ('group', 'slab'))]
    pallas_call x0 -> x2, Pallas kernels: none -> 82.3 us  [the longest x1 78.9 us: section(): pl.pallas_call(section_kernel, in_specs=[any_space] * 4 + [pl.BlockSpec(m...]
    another operation x15 -> x0, other arithmetic: 63.4 us -> none  [the longest x6 38.5 us: solve_coeffs(): chol = jnp.linalg.cholesky(gram)]
    slice x17 -> x0, local copies, waits for them, and re-layouts: 47.1 us -> none  [the longest x8 29.8 us: shift_y(): return jnp.roll(velocity, -offset, axis=2)]
    dot_general x4 -> x0, matrix products: 37.9 us -> none  [the longest x3 28.9 us: inner(): lax.dot_general(left, right, (((1,), (1,)), ((), ())), precision=lax.Prec...]
    add x1 -> x0, other arithmetic: 34.3 us -> none  [local(): new_velocity = velocity + section_gain * new_register]
  transfers between devices with their start and end apart: 4 -> 0, of which waited for: 1 -> 0; matrix products, arithmetic and copies ran while one was open for 24% -> 0% of each run, Pallas kernels for 0% -> 0%
where the time goes in v2:
time: 88.7 us; the launch traced here: 88.5 us
  Pallas kernels  82.3 us (93%)
  local copies, waits for them, and re-layouts  5.58 us (6%)
    pallas_call x1, Pallas kernels, section(): pl.pallas_call(section_kernel, in_specs=[any_space] * 4 + [pl.BlockSpec(m...  78.9 us
    unnamed x4, local copies, waits for them, and re-layouts  5.58 us
    pallas_call x1, Pallas kernels, finish(): pl.pallas_call(finish_kernel, out_shape=[jax.ShapeDtypeStruct((COUNT, RAN...  3.44 us

profile of v2, /device:TPU:1, one launch (start us, length us, event | category | flops | bytes accessed | tf_op | source)
XLA Modules:
  0.0 88.5 jit_solution(4961017916472621224)
XLA Ops:
  0.6 78.9 %section.1 = (f32[3,128,16,128]{3,2,1,0:T(8,128)}, f32[3,128,16,128]{3,2,1,0:T(8,128)}, f32[8,256]{1,0:T(8,128)}, f32[8,128]{1,0:T(8,128)}, f32[8,12288]{1,0:T(8,128)}) custom-call(f32[3,128,16,128]{3,2,1,0:T(8,128)} %bitcast.11, f32[3,128,16,128]{3,2,1,0:T(8,128)} %bitcast.12, f32[256,12288]{1,0:T(8,128)} %bitcast.8, f32[7,4,32,96]{3,2,1,0:T(8,128)} %past.1, ...), custom_call_target="tpu_custom_call" | custom-call | tf_op jit(solution)/shard_map/section/pallas_call | solution.py:507
  79.5 3.4 %finish.1 = (f32[8,256]{1,0:T(8,128)}, f32[8,8]{1,0:T(8,128)}, f32[8,12288]{1,0:T(8,128)}) custom-call(f32[8,256]{1,0:T(8,128)} %get-tuple-element.15.weights, f32[8,128]{1,0:T(8,128)} %get-tuple-element.16.wgram_ref, f32[8,12288]{1,0:T(8,128)} %get-tuple-element.17.residual), custom_call_target="tpu_custom_call" | custom-call | tf_op jit(solution)/shard_map/finish/pallas_call | solution.py:560
  82.9 0.0 copy-start
  82.9 3.9 %copy.12 = f32[3,128,128,16]{2,3,1,0:T(8,128)} copy(f32[3,128,128,16]{2,3,1,0:T(8,128)} %bitcast.10) | data formatting | bytes 6291456
  86.9 0.0 copy-done
  86.9 1.7 %copy.13 = f32[3,128,128,16]{2,3,1,0:T(8,128)} copy(f32[3,128,128,16]{2,3,1,0:T(8,128)S(1)} %bitcast.9) | data formatting | bytes 6291456
Async XLA Ops:
  82.9 3.9 %copy-start = (f32[3,128,16,128]{3,2,1,0:T(8,128)S(1)}, f32[3,128,16,128]{3,2,1,0:T(8,128)}, u32[]{:S(2)}) copy-start(f32[3,128,16,128]{3,2,1,0:T(8,128)} %get-tuple-element.14) | copy-start | bytes 9437188

commit v3 on v2

--- a/solution.py
+++ b/solution.py
@@ -25,6 +25,8 @@
 N_SLAB = 16
 N_POLE = 8
 N_PLANE = 16
+N_WALL = 32
+N_RING = 4
 RANK = 256
 ROWS = 12288
 COUNT = 8
@@ -32,7 +34,7 @@
 LANES = 384
 CHUNK = 1024
 N_CHUNK = ROWS // CHUNK
-BAND = RANK // N_SLAB
+BAND = RANK // N_WALL
 X_CHUNK = 16
 N_X = 128 // X_CHUNK
 BLOCK = 32
@@ -50,13 +52,33 @@
     return high, (value - high.astype(F32)).astype(BF16)
 
 
+def product(left, right, dims):
+    def parts(value):
+        high, rest = value.astype(BF16), value - value.astype(BF16).astype(F32)
+        middle = rest.astype(BF16)
+        return high, middle, (rest - middle.astype(F32)).astype(BF16)
+
+    (a, b, c), (d, e, f) = parts(left), parts(right)
+    (over_left,), (over_right,) = dims[0]
+    return dot(
+        jnp.concatenate([a, a, b, b, a, c], axis=over_left),
+        jnp.concatenate([d, e, d, e, f, d], axis=over_right),
+        dims,
+    )
+
+
 def peer(axis, step):
     group, slab = lax.axis_index("group"), lax.axis_index("slab")
     if axis == "group":
         return (lax.rem(group + step, N_GROUP), slab)
-    if axis == "slab":
-        return (group, lax.rem(slab + step, N_SLAB))
     column = lax.rem(slab // 2, 2)
+    if axis == "wall":
+        place = lax.rem(wall_index() + step, N_WALL)
+        within = lax.rem(place, N_POLE)
+        return (group // 4 * 4 + place // N_POLE, within // 2 * 4 + column * 2 + lax.rem(within, 2))
+    if axis == "ring":
+        place = lax.rem(ring_index() + step, N_RING)
+        return (place // 2 * 4 + lax.rem(group, 4), slab - column * 2 + lax.rem(place, 2) * 2)
     if axis == "pole":
         place = lax.rem(pole_index() + step, N_POLE)
         return (group, place // 2 * 4 + column * 2 + lax.rem(place, 2))
@@ -69,6 +91,14 @@
     return slab // 4 * 2 + lax.rem(slab, 2)
 
 
+def wall_index():
+    return lax.rem(lax.axis_index("group"), 4) * N_POLE + pole_index()
+
+
+def ring_index():
+    return lax.axis_index("group") // 4 * 2 + lax.rem(lax.axis_index("slab") // 2, 2)
+
+
 def plane_index():
     return lax.axis_index("group") * 2 + lax.rem(lax.axis_index("slab") // 2, 2)
 
@@ -81,7 +111,7 @@
 
 def hello():
     barrier = pltpu.get_barrier_semaphore()
-    for axis, size in (("slab", N_SLAB), ("plane", N_PLANE)):
+    for axis, size in (("plane", N_PLANE), ("wall", N_WALL)):
 
         def signal(step, carry, axis=axis):
             pl.semaphore_signal(barrier, inc=1, device_id=peer(axis, step))
@@ -93,7 +123,7 @@
 
 
 def everyone_in():
-    pl.semaphore_wait(pltpu.get_barrier_semaphore(), N_SLAB + N_PLANE)
+    pl.semaphore_wait(pltpu.get_barrier_semaphore(), N_WALL + N_PLANE)
 
 
 def broadcast(axis, size, source, target, send_sem, recv_sem):
@@ -174,9 +204,9 @@
         inverse = sweep_block(diagonal)[:, :BLOCK]
         inside = (lane >= start) & (lane < start + BLOCK)
         eye = jnp.where(lane - start == row, -1.0, 0.0)
-        solved = dot(inverse, jnp.where(inside, eye, panel), NN, HIGH)
+        solved = product(inverse, jnp.where(inside, eye, panel), NN)
         inside = (wide >= start) & (wide < start + BLOCK)
-        matrix[...] = jnp.where(inside, 0.0, matrix[...]) - dot(panel, solved, TN, HIGH)
+        matrix[...] = jnp.where(inside, 0.0, matrix[...]) - product(panel, solved, TN)
         matrix[start : start + BLOCK, :] = solved
 
 
@@ -231,15 +261,13 @@
 
 def section_kernel(
     velocity, register, basis, past, owner,
-    out_v, out_r, weights, wgram, sheet,
-    field, reg, new_v, edge_low, edge_high, low, high, blocks, top, rest, past_v, pieces, ship, rows,
-    local, partial, shares, groups, band, full, matrix, sums_ref, fresh, fresh_ship, fresh_in,
+    new_v, reg, weights, wgram, sheet,
+    field, edge_low, edge_high, low, high, blocks, top, rest, past_v, pieces, ship, rows,
+    local, partial, shares, rings, band, full, matrix, sums_ref, fresh, fresh_ship, fresh_in,
     proj_pole, proj_plane, res_pole, res_plane,
     field_sem, reg_sem, halo_send, halo_recv, block_sem, past_sem, piece_send, piece_recv, sum_send, sum_recv,
-    out_sem,
 ):
-    group, slab = lax.axis_index("group"), lax.axis_index("slab")
-    hello()
+    group = lax.axis_index("group")
 
     def part_of(chunk):
         return pl.ds(pl.multiple_of(chunk * X_CHUNK, X_CHUNK), X_CHUNK)
@@ -266,9 +294,10 @@
         lax.fori_loop(0, count, begin, 0)
 
     start_each(N_X, field_load)
+    hello()
     past_load = pltpu.make_async_copy(past, past_v, past_sem)
+    start_each(N_CHUNK, block_load)
     past_load.start()
-    start_each(N_CHUNK, block_load)
     start_each(N_X, reg_load)
 
     def halo(chunk, side):
@@ -295,29 +324,6 @@
         return carry
 
     lax.fori_loop(0, N_X, face, 0)
-    everyone_in()
-    lax.fori_loop(0, N_X, face_send, 0)
-
-    past_load.wait()
-    pieces[...] = jnp.zeros_like(pieces)
-
-    def arrange(place, carry):
-        piece, plane = place // PLANES, lax.rem(place, PLANES)
-        parts = [past_v[:, plane, pl.ds(piece * 4 + j, 1), :].reshape(COUNT - 1, 96) for j in range(4)]
-        pieces[piece, plane, 0 : COUNT - 1, :] = jnp.concatenate(parts, axis=1)
-        return carry
-
-    lax.fori_loop(0, N_GROUP * PLANES, arrange, 0)
-
-    def pick(step, carry):
-        ship[step] = pieces[piece_of(owner, lax.rem(group + step, N_GROUP))]
-        return carry
-
-    lax.fori_loop(0, N_GROUP, pick, 0)
-    rows[:, group] = ship[0]
-    broadcast(
-        "group", N_GROUP, lambda step: ship.at[step], rows.at[:, group], piece_send.at[0], piece_recv.at[0]
-    )
 
     local[...] = jnp.zeros_like(local)
 
@@ -328,39 +334,66 @@
         local[...] += dot(upper, jnp.concatenate([upper, lower], axis=0), NT)
         return carry
 
-    lax.fori_loop(0, N_CHUNK, multiply, 0)
+    lax.fori_loop(0, GRAM_FIRST, multiply, 0)
+    everyone_in()
+    lax.fori_loop(0, AHEAD, face_send, 0)
+    lax.fori_loop(GRAM_FIRST, N_CHUNK, multiply, 0)
     cross = local[:, RANK:]
-    partial[...] = (local[:, :RANK] + cross + cross.T).reshape(N_SLAB, BAND, RANK)
+    partial[...] = (local[:, :RANK] + cross + cross.T).reshape(N_WALL, BAND, RANK)
+
+    wall, ring = wall_index(), ring_index()
 
     def gram_first():
         broadcast(
-            "slab", N_SLAB, lambda step: partial.at[lax.rem(slab + step, N_SLAB)], shares.at[slab],
+            "wall", N_WALL, lambda step: partial.at[lax.rem(wall + step, N_WALL)], shares.at[wall],
             sum_send.at[0], sum_recv.at[0],
         )
-        shares[slab] = partial[slab]
+        shares[wall] = partial[wall]
 
     def gram_second():
-        drain(shares.at[pl.ds(0, N_SLAB - 1)], sum_recv.at[0])
-        groups[group] = add_slots(shares)
+        drain(shares.at[pl.ds(0, N_WALL - 1)], sum_recv.at[0])
+        rings[ring] = add_slots(shares)
         broadcast(
-            "group", N_GROUP, lambda step: groups.at[group], groups.at[group], sum_send.at[1], sum_recv.at[1]
+            "ring", N_RING, lambda step: rings.at[ring], rings.at[ring], sum_send.at[1], sum_recv.at[1]
         )
 
     def gram_third():
-        drain(groups.at[pl.ds(0, N_GROUP - 1)], sum_recv.at[1])
-        band[...] = add_slots(groups) * (1.0 / (ROWS * N_GROUP * N_SLAB))
-        full[slab] = band[...]
-        broadcast("slab", N_SLAB, lambda step: band, full.at[slab], sum_send.at[2], sum_recv.at[2])
-
-    def out_copy(chunk, which):
-        part = part_of(chunk)
-        source, target = ((new_v, out_v), (reg, out_r))[which]
-        return pltpu.make_async_copy(source.at[:, part], target.at[:, part], out_sem.at[which, chunk])
+        drain(rings.at[pl.ds(0, N_RING - 1)], sum_recv.at[1])
+        band[...] = add_slots(rings) * (1.0 / (ROWS * N_GROUP * N_SLAB))
+        full[wall] = band[...]
+        broadcast("wall", N_WALL, lambda step: band, full.at[wall], sum_send.at[2], sum_recv.at[2])
+
+    gram_first()
+
+    past_load.wait()
+    pieces[...] = jnp.zeros_like(pieces)
+
+    def arrange(place, carry):
+        piece, plane = place // PLANES, lax.rem(place, PLANES)
+        parts = [past_v[:, plane, pl.ds(piece * 4 + j, 1), :].reshape(COUNT - 1, 96) for j in range(4)]
+        pieces[piece, plane, 0 : COUNT - 1, :] = jnp.concatenate(parts, axis=1)
+        return carry
+
+    lax.fori_loop(0, N_GROUP * PLANES, arrange, 0)
+
+    def pick(step, carry):
+        ship[step] = pieces[piece_of(owner, lax.rem(group + step, N_GROUP))]
+        return carry
+
+    lax.fori_loop(0, N_GROUP, pick, 0)
+    rows[:, group] = ship[0]
+    broadcast(
+        "group", N_GROUP, lambda step: ship.at[step], rows.at[:, group], piece_send.at[0], piece_recv.at[0]
+    )
 
     def stencil(chunk, carry):
         halo(chunk, 0).wait_recv()
         halo(chunk, 1).wait_recv()
         reg_load(chunk).wait()
+
+        @pl.when(chunk + AHEAD < N_X)
+        def _():
+            face_send(chunk + AHEAD, 0)
 
         def coarse(quad, carry):
             x = chunk * X_CHUNK + quad * 4
@@ -375,11 +408,8 @@
             return carry
 
         lax.fori_loop(0, X_CHUNK // 4, coarse, 0)
-        out_copy(chunk, 0).start()
-        out_copy(chunk, 1).start()
-        return carry
-
-    gram_first()
+        return carry
+
     lax.fori_loop(0, SECOND_AT, stencil, 0)
     gram_second()
     lax.fori_loop(SECOND_AT, THIRD_AT, stencil, 0)
@@ -398,26 +428,37 @@
         "group", N_GROUP, lambda step: fresh_ship.at[step], fresh_in.at[group], piece_send.at[1], piece_recv.at[1]
     )
 
-    drain(full.at[pl.ds(0, N_SLAB - 1)], sum_recv.at[2])
-    matrix[...] = full[...].reshape(RANK, RANK)
-    invert(matrix, 0, 2)
-
     drain(ship.at[pl.ds(0, N_GROUP - 1)], piece_recv.at[0])
-    drain(fresh_ship.at[pl.ds(0, N_GROUP - 1)], piece_recv.at[1])
-    last = lax.broadcasted_iota(jnp.int32, (COUNT, LANES), 0) == COUNT - 1
-    for plane in range(PLANES):
-        for h in range(N_GROUP):
-            start = (plane * N_GROUP + h) * LANES
-            sheet[:, start : start + LANES] = jnp.where(
-                last, fresh_in[h, plane : plane + 1, :], rows[plane, h]
-            )
+    places = [(plane, h) for plane in range(PLANES) for h in range(N_GROUP)]
+    for at, (plane, h) in enumerate(places):
+        sheet[:, at * LANES : (at + 1) * LANES] = rows[plane, h]
 
     def project(step, total):
         head, tail = split(sheet[:, lanes_of(step)])
-        both = dot(jnp.concatenate([head, tail], axis=0), top[step], NT)
-        return total + both[:COUNT] + both[COUNT:] + dot(head, rest[step], NT)
-
-    proj = lax.fori_loop(0, N_CHUNK, project, jnp.zeros((COUNT, RANK), F32))
+        both = dot(top[step], jnp.concatenate([head, tail], axis=0), NT)
+        return total + both[:, :COUNT] + both[:, COUNT:] + dot(rest[step], head, NT)
+
+    past_proj = lax.fori_loop(0, N_CHUNK, project, jnp.zeros((RANK, COUNT), F32), unroll=4)
+
+    drain(full.at[pl.ds(0, N_WALL - 1)], sum_recv.at[2])
+    matrix[...] = full[...].reshape(RANK, RANK)
+    invert(matrix, 0, 1)
+
+    drain(fresh_ship.at[pl.ds(0, N_GROUP - 1)], piece_recv.at[1])
+    for at, (plane, h) in enumerate(places):
+        sheet[COUNT - 1 : COUNT, at * LANES : (at + 1) * LANES] = fresh_in[h, plane : plane + 1, :]
+
+    def project_fresh(step, total):
+        line = sheet[COUNT - 1 : COUNT, lanes_of(step)]
+        block = blocks[step]
+        for q in range(CHUNK // 128):
+            total = total + block[:, q * 128 : (q + 1) * 128] * line[:, q * 128 : (q + 1) * 128]
+        return total
+
+    fresh_proj = lax.fori_loop(0, N_CHUNK, project_fresh, jnp.zeros((RANK, 128), F32))
+    fresh_proj = jnp.sum(fresh_proj, axis=1, keepdims=True)
+    which = lax.broadcasted_iota(jnp.int32, (RANK, COUNT), 1)
+    proj = jnp.where(which == COUNT - 1, fresh_proj, past_proj).T
 
     def sum_first(value, pole_ref, place):
         pole = pole_index()
@@ -441,9 +482,9 @@
         return add_slots(plane_ref) * (1.0 / (ROWS * N_GROUP * N_SLAB))
 
     sum_first(proj, proj_pole, 3)
-    invert(matrix, 2, 4)
+    invert(matrix, 1, 3)
     sum_second(proj_pole, proj_plane, 3)
-    invert(matrix, 4, RANK // BLOCK)
+    invert(matrix, 3, RANK // BLOCK)
     proj = sum_end(proj_plane, 3)
     solved = -dot(proj, matrix[...], NN, HIGH)
     weights[...] = solved
@@ -458,21 +499,20 @@
         sheet[:, lanes_of(step)] = part
         return total + dot(part, part, NT, HIGH)
 
-    inner = lax.fori_loop(0, N_CHUNK, subtract, jnp.zeros((COUNT, COUNT), F32))
+    inner = lax.fori_loop(0, N_CHUNK, subtract, jnp.zeros((COUNT, COUNT), F32), unroll=4)
     sum_first(jnp.concatenate([inner, jnp.zeros((COUNT, 128 - COUNT), F32)], axis=1), res_pole, 5)
 
     def finish(chunk, carry):
         for which in range(2):
             halo(chunk, which).wait_send()
-            out_copy(chunk, which).wait()
         return carry
 
     lax.fori_loop(0, N_X, finish, 0)
     drain(ship.at[pl.ds(0, N_GROUP - 1)], piece_send.at[0])
     drain(fresh_ship.at[pl.ds(0, N_GROUP - 1)], piece_send.at[1])
-    drain(shares.at[pl.ds(0, N_SLAB - 1)], sum_send.at[0])
-    drain(groups.at[pl.ds(0, N_GROUP - 1)], sum_send.at[1])
-    drain(full.at[pl.ds(0, N_SLAB - 1)], sum_send.at[2])
+    drain(shares.at[pl.ds(0, N_WALL - 1)], sum_send.at[0])
+    drain(rings.at[pl.ds(0, N_RING - 1)], sum_send.at[1])
+    drain(full.at[pl.ds(0, N_WALL - 1)], sum_send.at[2])
     drain(proj_pole.at[pl.ds(0, N_POLE - 1)], sum_send.at[3])
     drain(proj_plane.at[pl.ds(0, N_PLANE - 1)], sum_send.at[4])
     sum_second(res_pole, res_plane, 5)
@@ -481,12 +521,13 @@
     drain(res_plane.at[pl.ds(0, N_PLANE - 1)], sum_send.at[6])
 
 
-SECOND_AT = 4
-THIRD_AT = 8
+AHEAD = 4
+GRAM_FIRST = 6
+SECOND_AT, THIRD_AT = 3, 6
 
 
 def section(velocity, register, basis, past, owner):
-    any_space = pl.BlockSpec(memory_space=pl.ANY)
+    hbm = pl.BlockSpec(memory_space=pltpu.HBM)
     vmem = pl.BlockSpec(memory_space=pltpu.VMEM)
     dma = pltpu.SemaphoreType.DMA
     field = (3, 128, 16, 128)
@@ -494,37 +535,40 @@
     pieces = (N_GROUP, PLANES, COUNT, LANES)
     fresh = (N_GROUP, PLANES, LANES)
     scratch = [
-        (field, F32), (field, F32), (field, F32), (face, F32), (face, F32), (face, F32), (face, F32),
+        (field, F32), (face, F32), (face, F32), (face, F32), (face, F32),
         ((N_CHUNK, RANK, CHUNK), F32), ((N_CHUNK, RANK, CHUNK), BF16), ((N_CHUNK, RANK, CHUNK), BF16),
         ((COUNT - 1, PLANES, 32, 96), F32), (pieces, F32), (pieces, F32), ((PLANES, N_GROUP, COUNT, LANES), F32),
-        ((RANK, 2 * RANK), F32), ((N_SLAB, BAND, RANK), F32), ((N_SLAB, BAND, RANK), F32),
-        ((N_GROUP, BAND, RANK), F32), ((BAND, RANK), F32), ((N_SLAB, BAND, RANK), F32), ((RANK, RANK), F32),
+        ((RANK, 2 * RANK), F32), ((N_WALL, BAND, RANK), F32), ((N_WALL, BAND, RANK), F32),
+        ((N_RING, BAND, RANK), F32), ((BAND, RANK), F32), ((N_WALL, BAND, RANK), F32), ((RANK, RANK), F32),
         ((1536, 128), F32), (fresh, F32), (fresh, F32), (fresh, F32),
         ((N_POLE, COUNT, RANK), F32), ((N_PLANE, COUNT, RANK), F32),
         ((N_POLE, COUNT, 128), F32), ((N_PLANE, COUNT, 128), F32),
     ]
-    semaphores = [(N_X,), (N_X,), (2, N_X), (2, N_X), (N_CHUNK,), None, (2,), (2,), (7,), (7,), (2, N_X)]
+    semaphores = [(N_X,), (N_X,), (2, N_X), (2, N_X), (N_CHUNK,), None, (2,), (2,), (7,), (7,)]
     return pl.pallas_call(
         section_kernel,
-        in_specs=[any_space] * 4 + [pl.BlockSpec(memory_space=pltpu.SMEM)],
-        out_specs=[any_space] * 2 + [vmem] * 3,
+        in_specs=[hbm] * 4 + [pl.BlockSpec(memory_space=pltpu.SMEM)],
+        out_specs=[vmem] * 5,
         out_shape=[
-            jax.ShapeDtypeStruct(field, F32),
-            jax.ShapeDtypeStruct(field, F32),
-            jax.ShapeDtypeStruct((COUNT, RANK), F32),
-            jax.ShapeDtypeStruct((COUNT, 128), F32),
-            jax.ShapeDtypeStruct((COUNT, ROWS), F32),
+            pltpu.VMEM(shape, F32)
+            for shape in (field, field, (COUNT, RANK), (COUNT, 128), (COUNT, ROWS))
         ],
         scratch_shapes=[pltpu.VMEM(shape, kind) for shape, kind in scratch]
         + [dma if shape is None else dma(shape) for shape in semaphores],
         compiler_params=pltpu.CompilerParams(
-            collective_id=0, has_side_effects=True, vmem_limit_bytes=58 * MIB
+            collective_id=0, has_side_effects=True, vmem_limit_bytes=46 * MIB
         ),
         name="section",
     )(velocity, register, basis, past, owner)
 
 
-def finish_kernel(weights, wgram_ref, residual, coeffs, factor, directions):
+def finish_kernel(new_v, reg, weights, wgram_ref, residual, out_v, out_r, coeffs, factor, directions, sems):
+    copies = [
+        pltpu.make_async_copy(source, target, sems.at[i])
+        for i, (source, target) in enumerate(((new_v, out_v), (reg, out_r)))
+    ]
+    for copy in copies:
+        copy.start()
     coeffs[...] = weights[...]
     wgram = wgram_ref[...]
     lane = lax.broadcasted_iota(jnp.int32, (COUNT, 128), 1)
@@ -554,25 +598,39 @@
         return carry
 
     lax.fori_loop(0, N_CHUNK, direct, 0)
-
-
-def finish(weights, wgram, residual):
+    for copy in copies:
+        copy.wait()
+
+
+def finish(*operands):
+    operands = [pltpu.with_memory_space_constraint(operand, pltpu.VMEM) for operand in operands]
+    vmem = pl.BlockSpec(memory_space=pltpu.VMEM)
     return pl.pallas_call(
         finish_kernel,
         out_shape=[
+            jax.ShapeDtypeStruct((3, 128, 16, 128), F32),
+            jax.ShapeDtypeStruct((3, 128, 16, 128), F32),
             jax.ShapeDtypeStruct((COUNT, RANK), F32),
             jax.ShapeDtypeStruct((COUNT, COUNT), F32),
             jax.ShapeDtypeStruct((COUNT, ROWS), F32),
         ],
+        in_specs=[vmem] * 5,
+        out_specs=[pl.BlockSpec(memory_space=pl.ANY)] * 2 + [vmem] * 3,
+        scratch_shapes=[pltpu.SemaphoreType.DMA((2,))],
+        compiler_params=pltpu.CompilerParams(vmem_limit_bytes=8 * MIB),
         name="finish",
-    )(weights, wgram, residual)
+    )(*operands)
 
 
 def local(velocity, register, past, basis, owner):
-    new_v, new_r, weights, wgram, residual = section(
-        velocity.transpose(0, 1, 3, 2), register.transpose(0, 1, 3, 2), basis.reshape(RANK, ROWS), past, owner.T
-    )
-    coeffs, factor, directions = finish(weights, wgram, residual)
+    operands = section(
+        velocity.transpose(0, 1, 3, 2),
+        register.transpose(0, 1, 3, 2),
+        basis.reshape(RANK, ROWS),
+        pltpu.with_memory_space_constraint(past, pltpu.HBM),
+        pltpu.with_memory_space_constraint(owner.T, pltpu.HBM),
+    )
+    new_v, new_r, coeffs, factor, directions = finish(*operands)
     return (
         new_v.transpose(0, 1, 3, 2),
         new_r.transpose(0, 1, 3, 2),

time: 88.7 us -> 73.2 us (0.83)
  Pallas kernels: 82.3 us -> 72.5 us
  local copies, waits for them, and re-layouts: 5.58 us -> 0 us
    pallas_call x2, Pallas kernels: 82.3 us -> 72.5 us  [the longest x1 69 us: section(): pl.pallas_call(section_kernel, in_specs=[hbm] * 4 + [pl.BlockSpec(memory_...]
    unnamed x4 -> x0, local copies, waits for them, and re-layouts: 5.58 us -> none
where the time goes in v3:
time: 73.2 us; the launch traced here: 73.1 us
  Pallas kernels  72.5 us (99%)
    pallas_call x1, Pallas kernels, section(): pl.pallas_call(section_kernel, in_specs=[hbm] * 4 + [pl.BlockSpec(memory_...  69 us
    pallas_call x1, Pallas kernels, finish(): pl.pallas_call(finish_kernel, out_shape=[jax.ShapeDtypeStruct((3, 128, 16...  3.47 us

profile of v3, /device:TPU:1, one launch (start us, length us, event | category | flops | bytes accessed | tf_op | source)
XLA Modules:
  0.0 73.1 jit_solution(737658502004343143)
XLA Ops:
  0.6 69.0 %section.1 = (f32[3,128,16,128]{3,2,1,0:T(8,128)S(1)}, f32[3,128,16,128]{3,2,1,0:T(8,128)S(1)}, f32[8,256]{1,0:T(8,128)S(1)}, f32[8,128]{1,0:T(8,128)S(1)}, f32[8,12288]{1,0:T(8,128)S(1)}) custom-call(f32[3,128,16,128]{3,2,1,0:T(8,128)} %bitcast.9, f32[3,128,16,128]{3,2,1,0:T(8,128)} %bitcast.10, f32[256,12288]{1,0:T(8,128)} %bitcast.8, ...), custom_call_target="tpu_custom_call" | custom-call | tf_op jit(solution)/shard_map/section/pallas_call | solution.py:548
  69.6 3.5 %finish.1 = (f32[3,128,16,128]{3,2,1,0:T(8,128)}, f32[3,128,16,128]{3,2,1,0:T(8,128)}, f32[8,256]{1,0:T(8,128)}, f32[8,8]{1,0:T(8,128)}, f32[8,12288]{1,0:T(8,128)}) custom-call(f32[3,128,16,128]{3,2,1,0:T(8,128)S(1)} %get-tuple-element.15.new_v, f32[3,128,16,128]{3,2,1,0:T(8,128)S(1)} %get-tuple-element.16.reg, f32[8,256]{1,0:T(8,128)S(1)} %get-tuple-element.17.weights, ...), custom_call_target="tpu_custom_call" | custom-call | tf_op jit(solution)/shard_map/finish/pallas_call | solution.py:608

commit v4 on v3

--- a/solution.py
+++ b/solution.py
@@ -52,13 +52,14 @@
     return high, (value - high.astype(F32)).astype(BF16)
 
 
+def in_parts(value):
+    high, rest = value.astype(BF16), value - value.astype(BF16).astype(F32)
+    middle = rest.astype(BF16)
+    return high, middle, (rest - middle.astype(F32)).astype(BF16)
+
+
 def product(left, right, dims):
-    def parts(value):
-        high, rest = value.astype(BF16), value - value.astype(BF16).astype(F32)
-        middle = rest.astype(BF16)
-        return high, middle, (rest - middle.astype(F32)).astype(BF16)
-
-    (a, b, c), (d, e, f) = parts(left), parts(right)
+    (a, b, c), (d, e, f) = in_parts(left), in_parts(right)
     (over_left,), (over_right,) = dims[0]
     return dot(
         jnp.concatenate([a, a, b, b, a, c], axis=over_left),
@@ -216,13 +217,19 @@
         rows = rows + sums_ref[pl.ds(z, 384, 4), :]
     row = lax.broadcasted_iota(jnp.int32, (512, 128), 0)
     lane = lax.broadcasted_iota(jnp.int32, (512, 128), 1)
-    fold = jnp.where((row // 128 == lane // 32) & ((row % 128) // 4 == lane % 32), 1 / 64, 0.0)
+    fold = jnp.where((row // 128 == lane // 32) & ((row % 128) // 4 == lane % 32), 1 / 64, 0.0).astype(BF16)
+    tiles = []
     for tile in range(3):
         parts = []
         for m in range(4):
             j, c = divmod(4 * tile + m, 3)
             parts.append(rows[(c * 4 + j) * 32 : (c * 4 + j) * 32 + 32])
-        part = dot(jnp.concatenate(parts, axis=1), fold.astype(F32), NN, HIGH)
+        tiles.append(jnp.concatenate(parts, axis=1))
+    boxes = jnp.concatenate(tiles, axis=0)
+    means = dot(jnp.concatenate(in_parts(boxes), axis=0), fold, NN)
+    means = means[:96] + (means[96:192] + means[192:])
+    for tile in range(3):
+        part = means[tile * 32 : (tile + 1) * 32]
         fresh[:, :, tile * 128 : (tile + 1) * 128] = part.reshape(N_GROUP, PLANES, 128)
 
 
@@ -336,7 +343,7 @@
 
     lax.fori_loop(0, GRAM_FIRST, multiply, 0)
     everyone_in()
-    lax.fori_loop(0, AHEAD, face_send, 0)
+    lax.fori_loop(0, FIRST, face_send, 0)
     lax.fori_loop(GRAM_FIRST, N_CHUNK, multiply, 0)
     cross = local[:, RANK:]
     partial[...] = (local[:, :RANK] + cross + cross.T).reshape(N_WALL, BAND, RANK)
@@ -364,6 +371,7 @@
         broadcast("wall", N_WALL, lambda step: band, full.at[wall], sum_send.at[2], sum_recv.at[2])
 
     gram_first()
+    lax.fori_loop(FIRST, AHEAD, face_send, 0)
 
     past_load.wait()
     pieces[...] = jnp.zeros_like(pieces)
@@ -382,14 +390,22 @@
 
     lax.fori_loop(0, N_GROUP, pick, 0)
     rows[:, group] = ship[0]
-    broadcast(
-        "group", N_GROUP, lambda step: ship.at[step], rows.at[:, group], piece_send.at[0], piece_recv.at[0]
-    )
-
-    def stencil(chunk, carry):
+
+    def ship_past():
+        broadcast(
+            "group", N_GROUP, lambda step: ship.at[step], rows.at[:, group], piece_send.at[0], piece_recv.at[0]
+        )
+
+    def arrive(chunk):
         halo(chunk, 0).wait_recv()
         halo(chunk, 1).wait_recv()
         reg_load(chunk).wait()
+
+    def stencil(chunk, carry):
+        arrive(chunk)
+        return advance(chunk, carry)
+
+    def advance(chunk, carry):
 
         @pl.when(chunk + AHEAD < N_X)
         def _():
@@ -414,7 +430,10 @@
     gram_second()
     lax.fori_loop(SECOND_AT, THIRD_AT, stencil, 0)
     gram_third()
-    lax.fori_loop(THIRD_AT, N_X, stencil, 0)
+    lax.fori_loop(THIRD_AT, N_X - 1, stencil, 0)
+    arrive(N_X - 1)
+    ship_past()
+    lax.fori_loop(N_X - 1, N_X, advance, 0)
 
     fold_fresh(sums_ref, fresh)
 
@@ -428,37 +447,26 @@
         "group", N_GROUP, lambda step: fresh_ship.at[step], fresh_in.at[group], piece_send.at[1], piece_recv.at[1]
     )
 
+    drain(full.at[pl.ds(0, N_WALL - 1)], sum_recv.at[2])
+    matrix[...] = full[...].reshape(RANK, RANK)
+    invert(matrix, 0, SWEPT[0])
+
     drain(ship.at[pl.ds(0, N_GROUP - 1)], piece_recv.at[0])
-    places = [(plane, h) for plane in range(PLANES) for h in range(N_GROUP)]
-    for at, (plane, h) in enumerate(places):
-        sheet[:, at * LANES : (at + 1) * LANES] = rows[plane, h]
+    drain(fresh_ship.at[pl.ds(0, N_GROUP - 1)], piece_recv.at[1])
+    last = lax.broadcasted_iota(jnp.int32, (COUNT, LANES), 0) == COUNT - 1
+    for plane in range(PLANES):
+        for h in range(N_GROUP):
+            start = (plane * N_GROUP + h) * LANES
+            sheet[:, start : start + LANES] = jnp.where(
+                last, fresh_in[h, plane : plane + 1, :], rows[plane, h]
+            )
 
     def project(step, total):
         head, tail = split(sheet[:, lanes_of(step)])
         both = dot(top[step], jnp.concatenate([head, tail], axis=0), NT)
         return total + both[:, :COUNT] + both[:, COUNT:] + dot(rest[step], head, NT)
 
-    past_proj = lax.fori_loop(0, N_CHUNK, project, jnp.zeros((RANK, COUNT), F32), unroll=4)
-
-    drain(full.at[pl.ds(0, N_WALL - 1)], sum_recv.at[2])
-    matrix[...] = full[...].reshape(RANK, RANK)
-    invert(matrix, 0, 1)
-
-    drain(fresh_ship.at[pl.ds(0, N_GROUP - 1)], piece_recv.at[1])
-    for at, (plane, h) in enumerate(places):
-        sheet[COUNT - 1 : COUNT, at * LANES : (at + 1) * LANES] = fresh_in[h, plane : plane + 1, :]
-
-    def project_fresh(step, total):
-        line = sheet[COUNT - 1 : COUNT, lanes_of(step)]
-        block = blocks[step]
-        for q in range(CHUNK // 128):
-            total = total + block[:, q * 128 : (q + 1) * 128] * line[:, q * 128 : (q + 1) * 128]
-        return total
-
-    fresh_proj = lax.fori_loop(0, N_CHUNK, project_fresh, jnp.zeros((RANK, 128), F32))
-    fresh_proj = jnp.sum(fresh_proj, axis=1, keepdims=True)
-    which = lax.broadcasted_iota(jnp.int32, (RANK, COUNT), 1)
-    proj = jnp.where(which == COUNT - 1, fresh_proj, past_proj).T
+    proj = lax.fori_loop(0, N_CHUNK, project, jnp.zeros((RANK, COUNT), F32), unroll=12).T
 
     def sum_first(value, pole_ref, place):
         pole = pole_index()
@@ -482,9 +490,9 @@
         return add_slots(plane_ref) * (1.0 / (ROWS * N_GROUP * N_SLAB))
 
     sum_first(proj, proj_pole, 3)
-    invert(matrix, 1, 3)
+    invert(matrix, SWEPT[0], SWEPT[1])
     sum_second(proj_pole, proj_plane, 3)
-    invert(matrix, 3, RANK // BLOCK)
+    invert(matrix, SWEPT[1], RANK // BLOCK)
     proj = sum_end(proj_plane, 3)
     solved = -dot(proj, matrix[...], NN, HIGH)
     weights[...] = solved
@@ -499,7 +507,7 @@
         sheet[:, lanes_of(step)] = part
         return total + dot(part, part, NT, HIGH)
 
-    inner = lax.fori_loop(0, N_CHUNK, subtract, jnp.zeros((COUNT, COUNT), F32), unroll=4)
+    inner = lax.fori_loop(0, N_CHUNK, subtract, jnp.zeros((COUNT, COUNT), F32), unroll=12)
     sum_first(jnp.concatenate([inner, jnp.zeros((COUNT, 128 - COUNT), F32)], axis=1), res_pole, 5)
 
     def finish(chunk, carry):
@@ -521,9 +529,10 @@
     drain(res_plane.at[pl.ds(0, N_PLANE - 1)], sum_send.at[6])
 
 
-AHEAD = 4
-GRAM_FIRST = 6
+FIRST, AHEAD = 3, 4
+GRAM_FIRST = 3
 SECOND_AT, THIRD_AT = 3, 6
+SWEPT = (3, 5)
 
 
 def section(velocity, register, basis, past, owner):
@@ -562,10 +571,11 @@
     )(velocity, register, basis, past, owner)
 
 
-def finish_kernel(new_v, reg, weights, wgram_ref, residual, out_v, out_r, coeffs, factor, directions, sems):
+def finish_kernel(new_v, reg, weights, wgram_ref, residual, out_v, out_r, coeffs, factor, out_d, directions, sems, last_sem):
     copies = [
-        pltpu.make_async_copy(source, target, sems.at[i])
-        for i, (source, target) in enumerate(((new_v, out_v), (reg, out_r)))
+        pltpu.make_async_copy(source.at[c], target.at[c], sems.at[which, c])
+        for which, (source, target) in enumerate(((new_v, out_v), (reg, out_r)))
+        for c in range(3)
     ]
     for copy in copies:
         copy.start()
@@ -598,6 +608,8 @@
         return carry
 
     lax.fori_loop(0, N_CHUNK, direct, 0)
+    copies.append(pltpu.make_async_copy(directions, out_d, last_sem))
+    copies[-1].start()
     for copy in copies:
         copy.wait()
 
@@ -605,6 +617,7 @@
 def finish(*operands):
     operands = [pltpu.with_memory_space_constraint(operand, pltpu.VMEM) for operand in operands]
     vmem = pl.BlockSpec(memory_space=pltpu.VMEM)
+    hbm = pl.BlockSpec(memory_space=pltpu.HBM)
     return pl.pallas_call(
         finish_kernel,
         out_shape=[
@@ -615,8 +628,12 @@
             jax.ShapeDtypeStruct((COUNT, ROWS), F32),
         ],
         in_specs=[vmem] * 5,
-        out_specs=[pl.BlockSpec(memory_space=pl.ANY)] * 2 + [vmem] * 3,
-        scratch_shapes=[pltpu.SemaphoreType.DMA((2,))],
+        out_specs=[hbm, hbm, vmem, vmem, hbm],
+        scratch_shapes=[
+            pltpu.VMEM((COUNT, ROWS), F32),
+            pltpu.SemaphoreType.DMA((2, 3)),
+            pltpu.SemaphoreType.DMA,
+        ],
         compiler_params=pltpu.CompilerParams(vmem_limit_bytes=8 * MIB),
         name="finish",
     )(*operands)

time: 73.2 us -> 70 us (0.956)
  Pallas kernels: 72.5 us -> 69.1 us
    pallas_call x1, Pallas kernels: 69 us -> 65.6 us  [section(): pl.pallas_call(section_kernel, in_specs=[hbm] * 4 + [pl.BlockSpec(memory_...]
where the time goes in v4:
time: 70 us; the launch traced here: 69.9 us
  Pallas kernels  69.1 us (99%)
  between operations  0.8 us (1%)
    pallas_call x1, Pallas kernels, section(): pl.pallas_call(section_kernel, in_specs=[hbm] * 4 + [pl.BlockSpec(memory_...  65.6 us
    pallas_call x1, Pallas kernels, finish(): pl.pallas_call(finish_kernel, out_shape=[jax.ShapeDtypeStruct((3, 128, 16...  3.42 us

profile of v4, /device:TPU:1, one launch (start us, length us, event | category | flops | bytes accessed | tf_op | source)
XLA Modules:
  0.0 69.9 jit_solution(1776422164441127749)
XLA Ops:
  0.6 65.6 %section.1 = (f32[3,128,16,128]{3,2,1,0:T(8,128)S(1)}, f32[3,128,16,128]{3,2,1,0:T(8,128)S(1)}, f32[8,256]{1,0:T(8,128)S(1)}, f32[8,128]{1,0:T(8,128)S(1)}, f32[8,12288]{1,0:T(8,128)S(1)}) custom-call(f32[3,128,16,128]{3,2,1,0:T(8,128)} %bitcast.9, f32[3,128,16,128]{3,2,1,0:T(8,128)} %bitcast.10, f32[256,12288]{1,0:T(8,128)} %bitcast.8, ...), custom_call_target="tpu_custom_call" | custom-call | tf_op jit(solution)/shard_map/section/pallas_call | solution.py:557
  66.3 3.4 %finish.1 = (f32[3,128,16,128]{3,2,1,0:T(8,128)}, f32[3,128,16,128]{3,2,1,0:T(8,128)}, f32[8,256]{1,0:T(8,128)}, f32[8,8]{1,0:T(8,128)}, f32[8,12288]{1,0:T(8,128)}) custom-call(f32[3,128,16,128]{3,2,1,0:T(8,128)S(1)} %get-tuple-element.15.new_v, f32[3,128,16,128]{3,2,1,0:T(8,128)S(1)} %get-tuple-element.16.reg, f32[8,256]{1,0:T(8,128)S(1)} %get-tuple-element.17.weights, ...), custom_call_target="tpu_custom_call" | custom-call | tf_op jit(solution)/shard_map/finish/pallas_call | solution.py:621

commit v5 on v4

--- a/solution.py
+++ b/solution.py
@@ -505,9 +505,11 @@
         image = both[:COUNT] + both[COUNT:] + dot(head, rest[step], NN)
         part = sheet[:, lanes_of(step)] - image
         sheet[:, lanes_of(step)] = part
-        return total + dot(part, part, NT, HIGH)
-
-    inner = lax.fori_loop(0, N_CHUNK, subtract, jnp.zeros((COUNT, COUNT), F32), unroll=12)
+        return total
+
+    lax.fori_loop(0, N_CHUNK, subtract, 0, unroll=12)
+    residual = sheet[...]
+    inner = dot(residual, residual, NT, HIGH)
     sum_first(jnp.concatenate([inner, jnp.zeros((COUNT, 128 - COUNT), F32)], axis=1), res_pole, 5)
 
     def finish(chunk, carry):
@@ -530,8 +532,8 @@
 
 
 FIRST, AHEAD = 3, 4
-GRAM_FIRST = 3
-SECOND_AT, THIRD_AT = 3, 6
+GRAM_FIRST = 4
+SECOND_AT, THIRD_AT = 3, 5
 SWEPT = (3, 5)
 
 

time: 70 us -> 68.6 us (0.980)
  Pallas kernels: 69.1 us -> 67.8 us
    pallas_call x1, Pallas kernels: 65.6 us -> 64.4 us  [section(): pl.pallas_call(section_kernel, in_specs=[hbm] * 4 + [pl.BlockSpec(memory_...]
where the time goes in v5:
time: 68.6 us; the launch traced here: 68.5 us
  Pallas kernels  67.8 us (99%)
    pallas_call x1, Pallas kernels, section(): pl.pallas_call(section_kernel, in_specs=[hbm] * 4 + [pl.BlockSpec(memory_...  64.4 us
    pallas_call x1, Pallas kernels, finish(): pl.pallas_call(finish_kernel, out_shape=[jax.ShapeDtypeStruct((3, 128, 16...  3.42 us

profile of v5, /device:TPU:1, one launch (start us, length us, event | category | flops | bytes accessed | tf_op | source)
XLA Modules:
  0.0 68.5 jit_solution(10836959143700523524)
XLA Ops:
  0.6 64.4 %section.1 = (f32[3,128,16,128]{3,2,1,0:T(8,128)S(1)}, f32[3,128,16,128]{3,2,1,0:T(8,128)S(1)}, f32[8,256]{1,0:T(8,128)S(1)}, f32[8,128]{1,0:T(8,128)S(1)}, f32[8,12288]{1,0:T(8,128)S(1)}) custom-call(f32[3,128,16,128]{3,2,1,0:T(8,128)} %bitcast.9, f32[3,128,16,128]{3,2,1,0:T(8,128)} %bitcast.10, f32[256,12288]{1,0:T(8,128)} %bitcast.8, ...), custom_call_target="tpu_custom_call" | custom-call | tf_op jit(solution)/shard_map/section/pallas_call | solution.py:559
  65.1 3.4 %finish.1 = (f32[3,128,16,128]{3,2,1,0:T(8,128)}, f32[3,128,16,128]{3,2,1,0:T(8,128)}, f32[8,256]{1,0:T(8,128)}, f32[8,8]{1,0:T(8,128)}, f32[8,12288]{1,0:T(8,128)}) custom-call(f32[3,128,16,128]{3,2,1,0:T(8,128)S(1)} %get-tuple-element.15.new_v, f32[3,128,16,128]{3,2,1,0:T(8,128)S(1)} %get-tuple-element.16.reg, f32[8,256]{1,0:T(8,128)S(1)} %get-tuple-element.17.weights, ...), custom_call_target="tpu_custom_call" | custom-call | tf_op jit(solution)/shard_map/finish/pallas_call | solution.py:623
